TPU v7x, 256 devices: a whole 4x4x8 slice. The times are simulated.
256 devices in a mesh: ta: 64 (over z, y, x_hi), sa: 4 (over x_lo, core).
Axes of the slice: x: 4 (x_hi: 2, x_lo: 2; x = x_hi * 2 + x_lo), y: 4, z: 8, core: 2. Of those that a mesh axis runs over, the one named last changes fastest.
Arguments:
- even_modes: bfloat16 [16, 2, 4, 3, 64, 16, 128], P(None, None, None, None, 'ta', 'sa'), may hold values from -6 to 6
- hop_links: bfloat16 [2, 4, 2, 3, 3, 64, 16, 128], P(None, None, None, None, None, 'ta', 'sa'), may hold values from -3.5 to 3.5
- clover_inverse: float32 [2, 2, 6, 6, 64, 16, 128], P(None, None, None, None, 'ta', 'sa'), may hold values from -0.2 to 1
- momenta: int32 [16, 3], replicated, may hold values from -2 to 2
- mode_weights: float32 [16], replicated, may hold values from 0.5 to 2
- separations: int32 [64, 16], P('ta'), may hold values from 1 to 63
Outputs:
- odd_modes: bfloat16 [16, 2, 4, 3, 64, 16, 128], P(None, None, None, None, 'ta', 'sa')
- correlator: float32 [64, 16], P('ta')
All inputs are finite; a program needn't handle non-finite values.
Results may differ from a plain program's by a relative error of at most 0.0055.
Values may be sent and summed in bfloat16 or wider, within the bound.
A program may use at most 128 MiB of HBM per device.

v0:
```python
import math

import jax
import jax.numpy as jnp
from jax import lax
from jax.sharding import PartitionSpec as P

NMODE = 16
NMOM = 16
LS = 16


hop_kappa = 0.125
gamma_source = ((3, 2, 1, 0), (3, 2, 1, 0), (2, 3, 0, 1), (2, 3, 0, 1))
gamma_factor = ((3, 3, 2, 2), (1, 0, 0, 1), (3, 2, 2, 3), (0, 0, 0, 0))


def with_halo(cells, sides, width):
    for axis, dim in sides:
        count = lax.axis_size(axis)
        head = lax.slice_in_dim(cells, 0, width, axis=dim)
        tail = lax.slice_in_dim(cells, cells.shape[dim] - width, cells.shape[dim], axis=dim)
        cells = jnp.concatenate(
            [
                lax.ppermute(tail, axis, [(i, (i + 1) % count) for i in range(count)]),
                cells,
                lax.ppermute(head, axis, [((i + 1) % count, i) for i in range(count)]),
            ],
            axis=dim,
        )
    return cells


def times_factor(real_part, imag_part, factor_code):
    if factor_code == 0:
        return (real_part, imag_part)
    if factor_code == 1:
        return (-real_part, -imag_part)
    if factor_code == 2:
        return (-imag_part, real_part)
    return (imag_part, -real_part)


def apply_gamma(spinor, d):
    spin_rows = []
    for s in range(4):
        source_spin = gamma_source[d][s]
        a, b = times_factor(
            spinor[:, 0, source_spin], spinor[:, 1, source_spin], gamma_factor[d][s]
        )
        spin_rows.append(jnp.stack([a, b], axis=1))
    return jnp.stack(spin_rows, axis=2)


def spinor_parts(flat):
    return [
        [
            (flat[:, s * 3 + c].astype(jnp.float32), flat[:, 12 + s * 3 + c].astype(jnp.float32))
            for c in range(3)
        ]
        for s in range(4)
    ]


def color_rows(link, spin_cols, adjoint):
    result = []
    for a in range(3):
        out_real = None
        out_imag = None
        for b in range(3):
            if adjoint:
                link_real = link[0, b, a]
                link_imag = -link[1, b, a]
            else:
                link_real = link[0, a, b]
                link_imag = link[1, a, b]
            part_real, part_imag = spin_cols[b]
            term_real = link_real * part_real - link_imag * part_imag
            term_imag = link_real * part_imag + link_imag * part_real
            out_real = term_real if out_real is None else out_real + term_real
            out_imag = term_imag if out_imag is None else out_imag + term_imag
        result.append((out_real, out_imag))
    return result


def gamma_parts(spinor, d):
    return [
        [
            times_factor(
                spinor[gamma_source[d][s]][c][0],
                spinor[gamma_source[d][s]][c][1],
                gamma_factor[d][s],
            )
            for c in range(3)
        ]
        for s in range(4)
    ]


def parity_grid(t_values, z_values):
    half_row = LS // 2
    y_place = jnp.arange(LS * half_row, dtype=jnp.int32) // half_row
    return (t_values[:, None, None] + z_values[None, :, None] + y_place[None, None, :] + 1) % 2 == 1


def x_neighbours(even_field, odd_shift):
    shape = even_field.shape
    grouped = even_field.reshape(shape[:-1] + (LS, LS // 2))
    ahead_rows = jnp.roll(grouped, -1, axis=-1).reshape(shape)
    behind_rows = jnp.roll(grouped, 1, axis=-1).reshape(shape)
    return (
        jnp.where(odd_shift, ahead_rows, even_field),
        jnp.where(odd_shift, even_field, behind_rows),
    )


def meson_plane(even_part, odd_part, time_value, z_values, momenta):
    half_row = LS // 2
    column = jnp.arange(LS * half_row, dtype=jnp.int32)
    y_grid = (column // half_row)[None, :]
    z_grid = jnp.broadcast_to(z_values[:, None], y_grid.shape)
    x_half = (column % half_row)[None, :]
    even_place = 2 * x_half + (time_value + z_grid + y_grid) % 2
    odd_place = 2 * x_half + (time_value + z_grid + y_grid + 1) % 2
    x_place = jnp.concatenate([even_place.reshape(-1), odd_place.reshape(-1)])
    y_place = jnp.concatenate([y_grid.reshape(-1), y_grid.reshape(-1)])
    z_place = jnp.concatenate([z_grid.reshape(-1), z_grid.reshape(-1)])
    lead_shape = even_part.shape[:4]
    vectors = jnp.concatenate(
        [even_part.reshape(lead_shape + (-1,)), odd_part.reshape(lead_shape + (-1,))], axis=-1
    )
    mode_count = vectors.shape[0]
    wave_number = (
        momenta[:, 0:1] * x_place[None, :]
        + momenta[:, 1:2] * y_place[None, :]
        + momenta[:, 2:3] * z_place[None, :]
    ) % LS
    phase_angle = wave_number.astype(jnp.float32) * (2.0 * math.pi / LS)
    cosine = jnp.tile(jnp.cos(phase_angle), (1, 12))[:, None, :]
    sine_part = jnp.tile(jnp.sin(phase_angle), (1, 12))[:, None, :]
    flat_vectors = vectors.reshape(mode_count, 2, -1)
    mode_real = flat_vectors[:, 0].astype(jnp.float32)[None]
    mode_imag = flat_vectors[:, 1].astype(jnp.float32)[None]
    left_rows = jnp.stack(
        [mode_real * cosine - mode_imag * sine_part, -(mode_real * sine_part + mode_imag * cosine)]
    ).astype(jnp.bfloat16)
    width = left_rows.shape[-1]
    right_cols = jnp.stack([apply_gamma(vectors, k) for k in range(4)]).reshape(-1, width)
    product = lax.dot_general(
        left_rows.reshape(-1, width),
        right_cols,
        (((1,), (1,)), ((), ())),
        preferred_element_type=jnp.float32,
    )
    return product.reshape(2, NMOM, mode_count, 4, mode_count, 2)


def meson_layout(product):
    real_part = product[0, ..., 0] - product[1, ..., 1]
    imag_part = product[0, ..., 1] + product[1, ..., 0]
    return jnp.stack([real_part, imag_part]).transpose(0, 3, 1, 2, 4)


def pair_block(weighted, piece):
    return lax.dot_general(
        weighted,
        piece.astype(jnp.float32),
        (((1,), (1,)), ((), ())),
        precision=lax.Precision.HIGHEST,
    )


def body(even_modes, hop_links, clover_inverse, momenta, mode_weights, separations):
    mode_count = even_modes.shape[0]
    rows_t = even_modes.shape[4]
    rows_z = even_modes.shape[5]
    half_row = LS // 2
    time_count = lax.axis_size("ta")
    time_rank = lax.axis_index("ta")
    space_rank = lax.axis_index("sa")
    t_values = time_rank * rows_t + jnp.arange(rows_t, dtype=jnp.int32)
    z_values = space_rank * rows_z + jnp.arange(rows_z, dtype=jnp.int32)
    padded = with_halo(even_modes, (("ta", 4), ("sa", 5)), 1)
    local_t = jnp.arange(rows_t)
    ahead_sign = jnp.where(
        (time_rank == time_count - 1) & (local_t == rows_t - 1), -1.0, 1.0
    ).astype(jnp.bfloat16)[:, None, None]
    behind_sign = jnp.where((time_rank == 0) & (local_t == 0), -1.0, 1.0).astype(jnp.bfloat16)[
        :, None, None
    ]
    odd_shift = parity_grid(t_values, z_values)
    x_ahead, x_behind = x_neighbours(even_modes, odd_shift)
    forward = (
        x_ahead,
        jnp.roll(even_modes, -half_row, axis=6),
        padded[:, :, :, :, 1:-1, 2:],
        padded[:, :, :, :, 2:, 1:-1] * ahead_sign,
    )
    backward = (
        x_behind,
        jnp.roll(even_modes, half_row, axis=6),
        padded[:, :, :, :, 1:-1, :-2],
        padded[:, :, :, :, :-2, 1:-1] * behind_sign,
    )
    links = hop_links.reshape(2, 4, 2, 3, 3, -1).astype(jnp.float32)
    running = None
    for d in range(4):
        ahead_in = spinor_parts(forward[d].reshape(mode_count, 24, -1))
        behind_in = spinor_parts(backward[d].reshape(mode_count, 24, -1))
        ahead = [color_rows(links[0, d], ahead_in[s], False) for s in range(4)]
        behind = [color_rows(links[1, d], behind_in[s], True) for s in range(4)]
        ahead_gamma = gamma_parts(ahead, d)
        behind_gamma = gamma_parts(behind, d)
        terms = []
        for s in range(4):
            row = []
            for c in range(3):
                pair = []
                for q in range(2):
                    value = (
                        ahead[s][c][q]
                        - ahead_gamma[s][c][q]
                        + behind[s][c][q]
                        + behind_gamma[s][c][q]
                    )
                    if running is not None:
                        value = (
                            running[s][c][q]
                            + ahead[s][c][q]
                            - ahead_gamma[s][c][q]
                            + behind[s][c][q]
                            + behind_gamma[s][c][q]
                        )
                    pair.append(value)
                row.append(pair)
            terms.append(row)
        running = terms
    clover = clover_inverse.reshape(2, 2, 6, 6, -1)
    real_rows = [None] * 12
    imag_rows = [None] * 12
    for chir in range(2):
        for r in range(6):
            out_real = None
            out_imag = None
            for col in range(6):
                half_real = hop_kappa * running[2 * chir + col // 3][col % 3][0]
                half_imag = hop_kappa * running[2 * chir + col // 3][col % 3][1]
                clover_real = clover[chir, 0, r, col]
                clover_imag = clover[chir, 1, r, col]
                term_real = clover_real * half_real - clover_imag * half_imag
                term_imag = clover_real * half_imag + clover_imag * half_real
                out_real = term_real if out_real is None else out_real + term_real
                out_imag = term_imag if out_imag is None else out_imag + term_imag
            place = (2 * chir + r // 3) * 3 + r % 3
            real_rows[place] = out_real
            imag_rows[place] = out_imag
    odd_modes = (
        jnp.stack(real_rows + imag_rows, axis=1).astype(jnp.bfloat16).reshape(even_modes.shape)
    )
    even_slice = even_modes[:, :, :, :, 0]
    odd_slice = odd_modes[:, :, :, :, 0]
    time_value = t_values[0]

    def add_plane(z, running_sum):
        even_part = lax.dynamic_slice_in_dim(even_slice, z, 1, 4)
        odd_part = lax.dynamic_slice_in_dim(odd_slice, z, 1, 4)
        plane_z = lax.dynamic_slice_in_dim(z_values, z, 1, 0)
        return running_sum + meson_plane(even_part, odd_part, time_value, plane_z, momenta)

    zero_start = jnp.zeros((2, NMOM, mode_count, 4, mode_count, 2), jnp.float32)
    slices = [meson_layout(lax.fori_loop(0, rows_z, add_plane, zero_start))]
    partial_value = jnp.stack(slices)
    meson = lax.psum(partial_value, "sa").astype(jnp.bfloat16)
    pair_weights = mode_weights[:, None] * mode_weights[None, :]
    weighted = (lax.optimization_barrier(meson).astype(jnp.float32) * pair_weights).reshape(
        rows_t, -1
    )
    flat_fields = meson.reshape(rows_t, -1)
    total_t = rows_t * time_count
    raw_pairs = pair_block(weighted, lax.all_gather(flat_fields, "ta", axis=0, tiled=True))
    sink_index = (t_values[:, None] + separations) % total_t
    matches = sink_index[:, :, None] == jnp.arange(total_t, dtype=jnp.int32)[None, None, :]
    picked = jnp.sum(jnp.where(matches, raw_pairs[:, None, :], 0.0), axis=-1)
    correlator = picked * (1.0 / (16.0 * NMODE * NMOM * LS**3))
    return (odd_modes, correlator)


def solution(mesh):
    in_specs = (
        P(None, None, None, None, "ta", "sa", None),
        P(None, None, None, None, None, "ta", "sa", None),
        P(None, None, None, None, "ta", "sa", None),
        P(),
        P(),
        P("ta", None),
    )
    out_specs = (P(None, None, None, None, "ta", "sa", None), P("ta", None))
    return jax.shard_map(body, mesh=mesh, in_specs=in_specs, out_specs=out_specs, check_vma=False)
```

profile of v0, /device:TPU:8, one launch (start us, length us, event | category | flops | bytes accessed | tf_op | source)
XLA Modules:
  0.0 465.1 jit_solution(6182609597824247403)
XLA Ops:
  7.2 1.9 copy.321
  9.1 2.9 collective-permute-start.1
  12.6 2.8 copy.314
  15.5 4.0 fusion.1217
  19.5 2.8 fusion.1216
  22.9 7.4 %fusion.42 = (bf16[16,2,4,3,1,4,128]{0,6,5,3,2,1,4:T(8,128)(2,1)S(1)}, bf16[16,2,4,3,1,4,128]{0,6,5,3,2,1,4:T(8,128)(2,1)S(1)}) fusion(bf16[16,2,4,3,1,4,128]{0,6,5,3,2,1,4:T(8,128)(2,1)S(1)} %copy.314, bf16[16,2,4,3,1,4,16,7]{0,7,6,5,3,2,1,4:T(8,128)(2,1)} %get-tuple-element.662, bf16[16,2,4,3,1,4,16,1]{0,7,6,5,3,2,1,4:T(2,128)(2,1)} %get-tuple-element.660, ...), kind=kLoop, calls=%fused_computation.105 | loop fusion | flops 1966080 | bytes 1966592 | tf_op jit(solution)/shard_map/jit(_where)/select_n | solution.py:113
  30.3 1.4 fusion.1214
  32.5 1.2 fusion.1212
  36.6 1.3 fusion.1221
  59.3 1.5 fusion.1231
  76.6 1.6 copy.461
  78.2 1.6 copy.458
  79.8 1.6 copy.459
  81.4 1.6 copy.456
  83.7 1.6 copy.454
  87.4 1.6 copy.466
  89.0 1.6 copy.467
  90.6 1.6 copy.464
  92.2 1.6 copy.465
  93.8 1.6 copy.462
  95.3 1.6 copy.463
  101.7 1.4 fusion.1219
  103.1 1.3 broadcast_multiply_fusion
  104.6 1.3 broadcast_multiply_fusion.1
  106.8 1.9 collective-permute-start.2
  110.5 3.9 collective-permute-done.3
  114.4 1.1 collective-permute-done.2
  117.5 2.3 add_add_fusion.17
  120.1 1.7 add_add_fusion.12
  121.9 1.7 add_add_fusion.13
  124.0 1.8 add_add_fusion.14
  125.8 1.8 add_add_fusion.15
  127.6 1.8 add_add_fusion.16
  129.8 2.2 add_add_fusion.19
  132.0 1.8 add_add_fusion.18
  134.2 7.1 %constant_dynamic-update-slice_fusion.26 = (bf16[16,24,512]{2,0,1:T(8,128)(2,1)S(1)}, f32[16,1,512]{2,0,1:T(8,128)S(1)}, f32[16,1,512]{2,0,1:T(8,128)S(1)}, f32[...) fusion(f32[16,1,512]{2,0,1:T(8,128)S(1)} %get-tuple-element.552, ...), kind=kLoop, calls=%fused_computation.1297 | loop fusion | flops 7004159 | bytes 4317184
  144.4 1.5 constant_dynamic-update-slice_fusion.20
  153.7 1.2 copy.427
  154.9 104.2 %while.17 = (s32[]{:T(128)}, f32[2,16,16,4,16,2]{4,2,5,3,1,0:T(8,128)}, bf16[16,2,4,3,4,128]{5,3,0,2,1,4:T(4,128)(2,1)}, bf16[16,2,4,3,4,128]{5,3,0,2,1,4:T(4,12...) while((s32[]{:T(128)}, ...), condition=%wide.region_1.2_spmd.clone, body=%wide.region_0.1_spmd.clone.sunk | while | flops 421997696 | bytes 17263324 | solution.py:271
  160.0 1.9 subtract_convert_fusion.2
  165.5 1.9 stack.476
  167.3 2.1 pad_maximum_fusion.14
  170.2 1.8 stack.477
  174.9 5.7 %select_add_fusion.2 = f32[2,16,16,4,16,2]{4,2,5,3,1,0:T(8,128)} fusion(f32[2,16,16,4,16,2]{4,2,5,3,1,0:T(8,128)} %get-tuple-element.1168, bf16[1,16,16,3072]{3,2,1,0:T(8,128)(2,1)S(1)} %get-tuple-element.1126, bf16[1,16,16,3072]{3,2,1,0:T(8,128)(2,1)S(1)} %get-tuple-element.1127, pred[]{:T(512)S(6)} %compare.27, ...), kind=kOutput, calls=%fused_computation.6.clone.1 | convolution fusion | flops 412221440 | bytes 4456449 | tf_op jit(solution)/shard_map/while/body/eval_jaxpr/dot_general | solution.py:149
  185.8 1.9 subtract_convert_fusion.2
  191.2 1.9 stack.476
  193.1 2.1 pad_maximum_fusion.14
  196.0 1.8 stack.477
  200.6 6.1 %select_add_fusion.2 = f32[2,16,16,4,16,2]{4,2,5,3,1,0:T(8,128)} fusion(f32[2,16,16,4,16,2]{4,2,5,3,1,0:T(8,128)} %get-tuple-element.1168, bf16[1,16,16,3072]{3,2,1,0:T(8,128)(2,1)S(1)} %get-tuple-element.1126, bf16[1,16,16,3072]{3,2,1,0:T(8,128)(2,1)S(1)} %get-tuple-element.1127, pred[]{:T(512)S(6)} %compare.27, ...), kind=kOutput, calls=%fused_computation.6.clone.1 | convolution fusion | flops 412221440 | bytes 4456449 | tf_op jit(solution)/shard_map/while/body/eval_jaxpr/dot_general | solution.py:149
  211.9 1.9 subtract_convert_fusion.2
  217.4 1.9 stack.476
  219.2 2.1 pad_maximum_fusion.14
  222.1 1.8 stack.477
  226.8 6.1 %select_add_fusion.2 = f32[2,16,16,4,16,2]{4,2,5,3,1,0:T(8,128)} fusion(f32[2,16,16,4,16,2]{4,2,5,3,1,0:T(8,128)} %get-tuple-element.1168, bf16[1,16,16,3072]{3,2,1,0:T(8,128)(2,1)S(1)} %get-tuple-element.1126, bf16[1,16,16,3072]{3,2,1,0:T(8,128)(2,1)S(1)} %get-tuple-element.1127, pred[]{:T(512)S(6)} %compare.27, ...), kind=kOutput, calls=%fused_computation.6.clone.1 | convolution fusion | flops 412221440 | bytes 4456449 | tf_op jit(solution)/shard_map/while/body/eval_jaxpr/dot_general | solution.py:149
  238.1 1.9 subtract_convert_fusion.2
  243.5 1.9 stack.476
  245.4 2.1 pad_maximum_fusion.14
  248.3 1.8 stack.477
  252.9 6.1 %select_add_fusion.2 = f32[2,16,16,4,16,2]{4,2,5,3,1,0:T(8,128)} fusion(f32[2,16,16,4,16,2]{4,2,5,3,1,0:T(8,128)} %get-tuple-element.1168, bf16[1,16,16,3072]{3,2,1,0:T(8,128)(2,1)S(1)} %get-tuple-element.1126, bf16[1,16,16,3072]{3,2,1,0:T(8,128)(2,1)S(1)} %get-tuple-element.1127, pred[]{:T(512)S(6)} %compare.27, ...), kind=kOutput, calls=%fused_computation.6.clone.1 | convolution fusion | flops 412221440 | bytes 4456449 | tf_op jit(solution)/shard_map/while/body/eval_jaxpr/dot_general | solution.py:149
  259.1 1.3 fusion.46
  260.4 1.3 subtract_bitcast_fusion
  261.8 27.3 %all-reduce.2 = bf16[1,2,4,16,16,16]{5,4,2,3,1,0:T(8,128)(2,1)S(1)} all-reduce(f32[1,2,4,16,16,16]{5,4,2,3,1,0:T(8,128)S(1)} %maximum_bitcast_fusion.20), channel_id=1, replica_groups=mesh['ta'=64,'sa'=4] {'sa'}, use_global_device_ids=true, to_apply=%region_2.3 | all-reduce | flops 32768 | bytes 196608 | tf_op jit(solution)/shard_map/psum | solution.py:273
  292.0 154.2 %all-gather.3.cloned.1.call-done = bf16[64,1,32768]{2,1,0:T(2,128)(2,1)} async-done(((bf16[1,1,32768]{2,1,0:T(2,128)(2,1)}), bf16[64,1,32768]{2,1,0:T(2,128)(2,1)}) %all-gather.3.cloned.1.call-update) | async-done | bytes 4194320 | tf_op jit(solution)/shard_map/all_gather | solution.py:280
  446.2 11.1 %fusion.43 = f32[64]{0:T(128)S(1)} fusion(f32[32768,1]{0,1:T(1,128)S(1)} %reshape.189346, bf16[64,1,32768]{2,1,0:T(2,128)(2,1)} %all-gather.3.cloned.1.call-done), kind=kOutput, calls=%fused_computation.106 | convolution fusion | flops 25165824 | bytes 4325632 | tf_op jit(solution)/shard_map/dot_general | solution.py:165
  (627 shorter events, 114.0 us)
Async XLA Ops:
  7.2 439.0 %all-gather.3.cloned.1.call-start = ((), (), s32[]{:S(2)}) async-start(), calls=%async_computation | async-start | bytes 8519680 | tf_op jit(solution)/shard_map/all_gather | solution.py:280
  9.1 95.5 %collective-permute-start.1 = (bf16[16,2,4,3,1,4,128]{6,0,5,4,3,2,1:T(8,128)(2,1)}, bf16[16,2,4,3,1,4,128]{6,0,5,4,3,2,1:T(8,128)(2,1)}, u32[]{:S(2)}, u32[]{:S(2)}) collective-permute-start(bf16[16,2,4,3,1,4,128]{6,0,5,4,3,2,1:T(8,128)(2,1)} %copy.321), channel_id=1, source_target_pairs={{4,0},{8,4},{12,8},{16,12},{20,16},{24,20},{28,24},{32,28},{36,32}... | collective-permute-start | bytes 1179656 | tf_op jit(solution)/shard_map/ppermute | solution.py:27
  12.0 91.1 %collective-permute-start = (bf16[16,2,4,3,1,4,128]{6,0,5,4,3,2,1:T(8,128)(2,1)}, bf16[16,2,4,3,1,4,128]{6,0,5,4,3,2,1:T(8,128)(2,1)}, u32[]{:S(2)}, u32[]{:S(2)}) collective-permute-start(bf16[16,2,4,3,1,4,128]{6,0,5,4,3,2,1:T(8,128)(2,1)} %copy.321), channel_id=1, source_target_pairs={{0,4},{4,8},{8,12},{12,16},{16,20},{20,24},{24,28},{28,32},{32,36}... | collective-permute-start | bytes 1179656 | tf_op jit(solution)/shard_map/ppermute | solution.py:25
  47.0 36.0 %copy-start.3 = (bf16[16,1,512]{0,2,1:T(8,128)(2,1)S(1)}, bf16[16,1,512]{0,2,1:T(8,128)(2,1)}, u32[]{:S(2)}) copy-start(bf16[16,1,512]{0,2,1:T(8,128)(2,1)} %get-tuple-element.652) | copy-start | bytes 49156
  47.7 23.0 %copy-start.28 = (f32[2,3,3,512]{3,0,2,1:T(2,128)S(1)}, f32[2,3,3,512]{3,0,2,1:T(2,128)}, u32[]{:S(2)}) copy-start(f32[2,3,3,512]{3,0,2,1:T(2,128)} %get-tuple-element.877) | copy-start | bytes 110596
  47.7 23.6 %copy-start.27 = (f32[2,3,3,512]{3,0,2,1:T(2,128)S(1)}, f32[2,3,3,512]{3,0,2,1:T(2,128)}, u32[]{:S(2)}) copy-start(f32[2,3,3,512]{3,0,2,1:T(2,128)} %get-tuple-element.876) | copy-start | bytes 110596
  47.7 24.3 %copy-start.26 = (f32[2,3,3,512]{3,0,2,1:T(2,128)S(1)}, f32[2,3,3,512]{3,0,2,1:T(2,128)}, u32[]{:S(2)}) copy-start(f32[2,3,3,512]{3,0,2,1:T(2,128)} %get-tuple-element.875) | copy-start | bytes 110596
  48.4 37.6 %copy-start.4 = (bf16[16,1,512]{0,2,1:T(8,128)(2,1)S(1)}, bf16[16,1,512]{0,2,1:T(8,128)(2,1)}, u32[]{:S(2)}) copy-start(bf16[16,1,512]{0,2,1:T(8,128)(2,1)} %get-tuple-element.658) | copy-start | bytes 49156
  106.8 7.5 %collective-permute-start.3 = (bf16[16,2,4,3,3,1,128]{6,0,5,4,3,2,1:T(8,128)(2,1)}, bf16[16,2,4,3,3,1,128]{6,0,5,4,3,2,1:T(8,128)(2,1)S(1)}, u32[]{:S(2)}, u32[]{:S(2)}) collective-permute-start(bf16[16,2,4,3,3,1,128]{6,0,5,4,3,2,1:T(8,128)(2,1)} %get-tuple-element.666), channel_id=1, source_target_pairs={{0,1},{1,2},{2,3},{3,0},{4,5},{5,6},{6,7},{7,4},{8,9},{9,10},{10,1... | collective-permute-start | bytes 884744 | tf_op jit(solution)/shard_map/ppermute | solution.py:25
  106.8 8.6 %collective-permute-start.2 = (bf16[16,2,4,3,3,1,128]{6,0,5,4,3,2,1:T(8,128)(2,1)}, bf16[16,2,4,3,3,1,128]{6,0,5,4,3,2,1:T(8,128)(2,1)}, u32[]{:S(2)}, u32[]{:S(2)}) collective-permute-start(bf16[16,2,4,3,3,1,128]{6,0,5,4,3,2,1:T(8,128)(2,1)} %get-tuple-element.667), channel_id=1, source_target_pairs={{1,0},{2,1},{3,2},{0,3},{5,4},{6,5},{7,6},{4,7},{9,8},{10,9},{11,1... | collective-permute-start | bytes 884744 | tf_op jit(solution)/shard_map/ppermute | solution.py:27
  109.6 7.9 %copy-start.41 = (bf16[16,1,512]{2,1,0:T(2,128)(2,1)S(1)}, bf16[16,1,512]{2,1,0:T(2,128)(2,1)}, u32[]{:S(2)}) copy-start(bf16[16,1,512]{2,1,0:T(2,128)(2,1)} %get-tuple-element.697) | copy-start | bytes 49156
  109.6 7.9 %copy-start.42 = (bf16[16,1,512]{2,1,0:T(2,128)(2,1)S(1)}, bf16[16,1,512]{2,1,0:T(2,128)(2,1)}, u32[]{:S(2)}) copy-start(bf16[16,1,512]{2,1,0:T(2,128)(2,1)} %get-tuple-element.698) | copy-start | bytes 49156
  109.6 7.9 %copy-start.43 = (bf16[16,1,512]{2,1,0:T(2,128)(2,1)S(1)}, bf16[16,1,512]{2,1,0:T(2,128)(2,1)}, u32[]{:S(2)}) copy-start(bf16[16,1,512]{2,1,0:T(2,128)(2,1)} %get-tuple-element.699) | copy-start | bytes 49156
  109.6 7.9 %copy-start.44 = (bf16[16,1,512]{2,1,0:T(2,128)(2,1)S(1)}, bf16[16,1,512]{2,1,0:T(2,128)(2,1)}, u32[]{:S(2)}) copy-start(bf16[16,1,512]{2,1,0:T(2,128)(2,1)} %get-tuple-element.700) | copy-start | bytes 49156
  109.6 7.9 %copy-start.45 = (bf16[16,1,512]{2,1,0:T(2,128)(2,1)S(1)}, bf16[16,1,512]{2,1,0:T(2,128)(2,1)}, u32[]{:S(2)}) copy-start(bf16[16,1,512]{2,1,0:T(2,128)(2,1)} %get-tuple-element.701) | copy-start | bytes 49156
  109.6 7.9 %copy-start.46 = (bf16[16,1,512]{2,1,0:T(2,128)(2,1)S(1)}, bf16[16,1,512]{2,1,0:T(2,128)(2,1)}, u32[]{:S(2)}) copy-start(bf16[16,1,512]{2,1,0:T(2,128)(2,1)} %get-tuple-element.702) | copy-start | bytes 49156
  109.6 7.9 %copy-start.47 = (bf16[16,1,512]{2,1,0:T(2,128)(2,1)S(1)}, bf16[16,1,512]{2,1,0:T(2,128)(2,1)}, u32[]{:S(2)}) copy-start(bf16[16,1,512]{2,1,0:T(2,128)(2,1)} %get-tuple-element.703) | copy-start | bytes 49156
  109.6 7.9 %copy-start.48 = (bf16[16,1,512]{2,1,0:T(2,128)(2,1)S(1)}, bf16[16,1,512]{2,1,0:T(2,128)(2,1)}, u32[]{:S(2)}) copy-start(bf16[16,1,512]{2,1,0:T(2,128)(2,1)} %get-tuple-element.704) | copy-start | bytes 49156
  109.6 7.9 %copy-start.49 = (bf16[16,1,512]{2,1,0:T(2,128)(2,1)S(1)}, bf16[16,1,512]{2,1,0:T(2,128)(2,1)}, u32[]{:S(2)}) copy-start(bf16[16,1,512]{2,1,0:T(2,128)(2,1)} %get-tuple-element.705) | copy-start | bytes 49156
  109.7 7.9 %copy-start.50 = (bf16[16,1,512]{2,1,0:T(2,128)(2,1)S(1)}, bf16[16,1,512]{2,1,0:T(2,128)(2,1)}, u32[]{:S(2)}) copy-start(bf16[16,1,512]{2,1,0:T(2,128)(2,1)} %get-tuple-element.706) | copy-start | bytes 49156
  133.8 9.0 %copy-start.186 = (f32[1,1,1,1,512]{4,1,3,2,0:T(1,128)S(1)}, f32[1,1,1,1,512]{4,1,3,2,0:T(1,128)}, u32[]{:S(2)}) copy-start(f32[1,1,1,1,512]{4,1,3,2,0:T(1,128)} %get-tuple-element.824) | copy-start | bytes 6148
  133.8 9.0 %copy-start.187 = (f32[1,1,1,1,512]{4,1,3,2,0:T(1,128)S(1)}, f32[1,1,1,1,512]{4,1,3,2,0:T(1,128)}, u32[]{:S(2)}) copy-start(f32[1,1,1,1,512]{4,1,3,2,0:T(1,128)} %get-tuple-element.825) | copy-start | bytes 6148
  133.9 9.0 %copy-start.188 = (f32[1,1,1,1,512]{4,1,3,2,0:T(1,128)S(1)}, f32[1,1,1,1,512]{4,1,3,2,0:T(1,128)}, u32[]{:S(2)}) copy-start(f32[1,1,1,1,512]{4,1,3,2,0:T(1,128)} %get-tuple-element.826) | copy-start | bytes 6148
  133.9 9.0 %copy-start.189 = (f32[1,1,1,1,512]{4,1,3,2,0:T(1,128)S(1)}, f32[1,1,1,1,512]{4,1,3,2,0:T(1,128)}, u32[]{:S(2)}) copy-start(f32[1,1,1,1,512]{4,1,3,2,0:T(1,128)} %get-tuple-element.827) | copy-start | bytes 6148
  133.9 9.8 %copy-start.173 = (f32[1,1,1,1,512]{4,1,3,2,0:T(1,128)S(1)}, f32[1,1,1,1,512]{4,1,3,2,0:T(1,128)}, u32[]{:S(2)}) copy-start(f32[1,1,1,1,512]{4,1,3,2,0:T(1,128)} %get-tuple-element.820) | copy-start | bytes 6148
  133.9 9.8 %copy-start.174 = (f32[1,1,1,1,512]{4,1,3,2,0:T(1,128)S(1)}, f32[1,1,1,1,512]{4,1,3,2,0:T(1,128)}, u32[]{:S(2)}) copy-start(f32[1,1,1,1,512]{4,1,3,2,0:T(1,128)} %get-tuple-element.821) | copy-start | bytes 6148
  133.9 9.8 %copy-start.175 = (f32[1,1,1,1,512]{4,1,3,2,0:T(1,128)S(1)}, f32[1,1,1,1,512]{4,1,3,2,0:T(1,128)}, u32[]{:S(2)}) copy-start(f32[1,1,1,1,512]{4,1,3,2,0:T(1,128)} %get-tuple-element.822) | copy-start | bytes 6148
  133.9 9.8 %copy-start.176 = (f32[1,1,1,1,512]{4,1,3,2,0:T(1,128)S(1)}, f32[1,1,1,1,512]{4,1,3,2,0:T(1,128)}, u32[]{:S(2)}) copy-start(f32[1,1,1,1,512]{4,1,3,2,0:T(1,128)} %get-tuple-element.823) | copy-start | bytes 6148
  133.9 9.8 %copy-start.178 = (f32[1,1,1,1,512]{4,1,3,2,0:T(1,128)S(1)}, f32[1,1,1,1,512]{4,1,3,2,0:T(1,128)}, u32[]{:S(2)}) copy-start(f32[1,1,1,1,512]{4,1,3,2,0:T(1,128)} %get-tuple-element.812) | copy-start | bytes 6148
  133.9 9.8 %copy-start.179 = (f32[1,1,1,1,512]{4,1,3,2,0:T(1,128)S(1)}, f32[1,1,1,1,512]{4,1,3,2,0:T(1,128)}, u32[]{:S(2)}) copy-start(f32[1,1,1,1,512]{4,1,3,2,0:T(1,128)} %get-tuple-element.813) | copy-start | bytes 6148
  133.9 9.8 %copy-start.180 = (f32[1,1,1,1,512]{4,1,3,2,0:T(1,128)S(1)}, f32[1,1,1,1,512]{4,1,3,2,0:T(1,128)}, u32[]{:S(2)}) copy-start(f32[1,1,1,1,512]{4,1,3,2,0:T(1,128)} %get-tuple-element.814) | copy-start | bytes 6148
  133.9 9.8 %copy-start.181 = (f32[1,1,1,1,512]{4,1,3,2,0:T(1,128)S(1)}, f32[1,1,1,1,512]{4,1,3,2,0:T(1,128)}, u32[]{:S(2)}) copy-start(f32[1,1,1,1,512]{4,1,3,2,0:T(1,128)} %get-tuple-element.815) | copy-start | bytes 6148
  134.0 9.8 %copy-start.182 = (f32[1,1,1,1,512]{4,1,3,2,0:T(1,128)S(1)}, f32[1,1,1,1,512]{4,1,3,2,0:T(1,128)}, u32[]{:S(2)}) copy-start(f32[1,1,1,1,512]{4,1,3,2,0:T(1,128)} %get-tuple-element.816) | copy-start | bytes 6148
  134.0 9.8 %copy-start.183 = (f32[1,1,1,1,512]{4,1,3,2,0:T(1,128)S(1)}, f32[1,1,1,1,512]{4,1,3,2,0:T(1,128)}, u32[]{:S(2)}) copy-start(f32[1,1,1,1,512]{4,1,3,2,0:T(1,128)} %get-tuple-element.817) | copy-start | bytes 6148
  134.0 9.8 %copy-start.184 = (f32[1,1,1,1,512]{4,1,3,2,0:T(1,128)S(1)}, f32[1,1,1,1,512]{4,1,3,2,0:T(1,128)}, u32[]{:S(2)}) copy-start(f32[1,1,1,1,512]{4,1,3,2,0:T(1,128)} %get-tuple-element.818) | copy-start | bytes 6148
  134.0 9.8 %copy-start.185 = (f32[1,1,1,1,512]{4,1,3,2,0:T(1,128)S(1)}, f32[1,1,1,1,512]{4,1,3,2,0:T(1,128)}, u32[]{:S(2)}) copy-start(f32[1,1,1,1,512]{4,1,3,2,0:T(1,128)} %get-tuple-element.819) | copy-start | bytes 6148
  134.0 9.9 %copy-start.162 = (f32[1,1,1,1,512]{4,1,3,2,0:T(1,128)S(1)}, f32[1,1,1,1,512]{4,1,3,2,0:T(1,128)}, u32[]{:S(2)}) copy-start(f32[1,1,1,1,512]{4,1,3,2,0:T(1,128)} %get-tuple-element.801) | copy-start | bytes 6148
  134.0 9.9 %copy-start.163 = (f32[1,1,1,1,512]{4,1,3,2,0:T(1,128)S(1)}, f32[1,1,1,1,512]{4,1,3,2,0:T(1,128)}, u32[]{:S(2)}) copy-start(f32[1,1,1,1,512]{4,1,3,2,0:T(1,128)} %get-tuple-element.802) | copy-start | bytes 6148
  134.0 9.9 %copy-start.164 = (f32[1,1,1,1,512]{4,1,3,2,0:T(1,128)S(1)}, f32[1,1,1,1,512]{4,1,3,2,0:T(1,128)}, u32[]{:S(2)}) copy-start(f32[1,1,1,1,512]{4,1,3,2,0:T(1,128)} %get-tuple-element.803) | copy-start | bytes 6148
  134.0 9.9 %copy-start.165 = (f32[1,1,1,1,512]{4,1,3,2,0:T(1,128)S(1)}, f32[1,1,1,1,512]{4,1,3,2,0:T(1,128)}, u32[]{:S(2)}) copy-start(f32[1,1,1,1,512]{4,1,3,2,0:T(1,128)} %get-tuple-element.804) | copy-start | bytes 6148
  134.0 9.9 %copy-start.166 = (f32[1,1,1,1,512]{4,1,3,2,0:T(1,128)S(1)}, f32[1,1,1,1,512]{4,1,3,2,0:T(1,128)}, u32[]{:S(2)}) copy-start(f32[1,1,1,1,512]{4,1,3,2,0:T(1,128)} %get-tuple-element.805) | copy-start | bytes 6148
  134.0 9.9 %copy-start.167 = (f32[1,1,1,1,512]{4,1,3,2,0:T(1,128)S(1)}, f32[1,1,1,1,512]{4,1,3,2,0:T(1,128)}, u32[]{:S(2)}) copy-start(f32[1,1,1,1,512]{4,1,3,2,0:T(1,128)} %get-tuple-element.806) | copy-start | bytes 6148
  134.1 9.9 %copy-start.168 = (f32[1,1,1,1,512]{4,1,3,2,0:T(1,128)S(1)}, f32[1,1,1,1,512]{4,1,3,2,0:T(1,128)}, u32[]{:S(2)}) copy-start(f32[1,1,1,1,512]{4,1,3,2,0:T(1,128)} %get-tuple-element.807) | copy-start | bytes 6148
  134.1 9.9 %copy-start.169 = (f32[1,1,1,1,512]{4,1,3,2,0:T(1,128)S(1)}, f32[1,1,1,1,512]{4,1,3,2,0:T(1,128)}, u32[]{:S(2)}) copy-start(f32[1,1,1,1,512]{4,1,3,2,0:T(1,128)} %get-tuple-element.808) | copy-start | bytes 6148
  134.1 9.9 %copy-start.170 = (f32[1,1,1,1,512]{4,1,3,2,0:T(1,128)S(1)}, f32[1,1,1,1,512]{4,1,3,2,0:T(1,128)}, u32[]{:S(2)}) copy-start(f32[1,1,1,1,512]{4,1,3,2,0:T(1,128)} %get-tuple-element.809) | copy-start | bytes 6148
  134.1 9.9 %copy-start.171 = (f32[1,1,1,1,512]{4,1,3,2,0:T(1,128)S(1)}, f32[1,1,1,1,512]{4,1,3,2,0:T(1,128)}, u32[]{:S(2)}) copy-start(f32[1,1,1,1,512]{4,1,3,2,0:T(1,128)} %get-tuple-element.810) | copy-start | bytes 6148
  134.1 9.9 %copy-start.172 = (f32[1,1,1,1,512]{4,1,3,2,0:T(1,128)S(1)}, f32[1,1,1,1,512]{4,1,3,2,0:T(1,128)}, u32[]{:S(2)}) copy-start(f32[1,1,1,1,512]{4,1,3,2,0:T(1,128)} %get-tuple-element.811) | copy-start | bytes 6148
  134.1 9.9 %copy-start.177 = (f32[1,1,1,1,512]{4,1,3,2,0:T(1,128)S(1)}, f32[1,1,1,1,512]{4,1,3,2,0:T(1,128)}, u32[]{:S(2)}) copy-start(f32[1,1,1,1,512]{4,1,3,2,0:T(1,128)} %get-tuple-element.800) | copy-start | bytes 6148
  134.1 9.9 %copy-start.95 = (f32[1,1,1,1,512]{4,1,3,2,0:T(1,128)S(1)}, f32[1,1,1,1,512]{4,1,3,2,0:T(1,128)}, u32[]{:S(2)}) copy-start(f32[1,1,1,1,512]{4,1,3,2,0:T(1,128)} %get-tuple-element.788) | copy-start | bytes 6148
  134.1 9.9 %copy-start.96 = (f32[1,1,1,1,512]{4,1,3,2,0:T(1,128)S(1)}, f32[1,1,1,1,512]{4,1,3,2,0:T(1,128)}, u32[]{:S(2)}) copy-start(f32[1,1,1,1,512]{4,1,3,2,0:T(1,128)} %get-tuple-element.789) | copy-start | bytes 6148
  134.1 9.9 %copy-start.97 = (f32[1,1,1,1,512]{4,1,3,2,0:T(1,128)S(1)}, f32[1,1,1,1,512]{4,1,3,2,0:T(1,128)}, u32[]{:S(2)}) copy-start(f32[1,1,1,1,512]{4,1,3,2,0:T(1,128)} %get-tuple-element.790) | copy-start | bytes 6148
  134.1 9.9 %copy-start.98 = (f32[1,1,1,1,512]{4,1,3,2,0:T(1,128)S(1)}, f32[1,1,1,1,512]{4,1,3,2,0:T(1,128)}, u32[]{:S(2)}) copy-start(f32[1,1,1,1,512]{4,1,3,2,0:T(1,128)} %get-tuple-element.791) | copy-start | bytes 6148
  134.2 9.9 %copy-start.99 = (f32[1,1,1,1,512]{4,1,3,2,0:T(1,128)S(1)}, f32[1,1,1,1,512]{4,1,3,2,0:T(1,128)}, u32[]{:S(2)}) copy-start(f32[1,1,1,1,512]{4,1,3,2,0:T(1,128)} %get-tuple-element.792) | copy-start | bytes 6148
  134.2 9.9 %copy-start.100 = (f32[1,1,1,1,512]{4,1,3,2,0:T(1,128)S(1)}, f32[1,1,1,1,512]{4,1,3,2,0:T(1,128)}, u32[]{:S(2)}) copy-start(f32[1,1,1,1,512]{4,1,3,2,0:T(1,128)} %get-tuple-element.793) | copy-start | bytes 6148
  134.2 9.9 %copy-start.101 = (f32[1,1,1,1,512]{4,1,3,2,0:T(1,128)S(1)}, f32[1,1,1,1,512]{4,1,3,2,0:T(1,128)}, u32[]{:S(2)}) copy-start(f32[1,1,1,1,512]{4,1,3,2,0:T(1,128)} %get-tuple-element.794) | copy-start | bytes 6148
  134.2 9.9 %copy-start.102 = (f32[1,1,1,1,512]{4,1,3,2,0:T(1,128)S(1)}, f32[1,1,1,1,512]{4,1,3,2,0:T(1,128)}, u32[]{:S(2)}) copy-start(f32[1,1,1,1,512]{4,1,3,2,0:T(1,128)} %get-tuple-element.795) | copy-start | bytes 6148
  134.2 9.9 %copy-start.103 = (f32[1,1,1,1,512]{4,1,3,2,0:T(1,128)S(1)}, f32[1,1,1,1,512]{4,1,3,2,0:T(1,128)}, u32[]{:S(2)}) copy-start(f32[1,1,1,1,512]{4,1,3,2,0:T(1,128)} %get-tuple-element.796) | copy-start | bytes 6148
  134.2 9.9 %copy-start.104 = (f32[1,1,1,1,512]{4,1,3,2,0:T(1,128)S(1)}, f32[1,1,1,1,512]{4,1,3,2,0:T(1,128)}, u32[]{:S(2)}) copy-start(f32[1,1,1,1,512]{4,1,3,2,0:T(1,128)} %get-tuple-element.797) | copy-start | bytes 6148
  134.2 9.9 %copy-start.105 = (f32[1,1,1,1,512]{4,1,3,2,0:T(1,128)S(1)}, f32[1,1,1,1,512]{4,1,3,2,0:T(1,128)}, u32[]{:S(2)}) copy-start(f32[1,1,1,1,512]{4,1,3,2,0:T(1,128)} %get-tuple-element.798) | copy-start | bytes 6148
  134.2 9.9 %copy-start.106 = (f32[1,1,1,1,512]{4,1,3,2,0:T(1,128)S(1)}, f32[1,1,1,1,512]{4,1,3,2,0:T(1,128)}, u32[]{:S(2)}) copy-start(f32[1,1,1,1,512]{4,1,3,2,0:T(1,128)} %get-tuple-element.799) | copy-start | bytes 6148
  146.0 7.3 %copy-start.135 = (f32[1,1,1,1,512]{4,1,3,2,0:T(1,128)S(1)}, f32[1,1,1,1,512]{4,1,3,2,0:T(1,128)}, u32[]{:S(2)}) copy-start(f32[1,1,1,1,512]{4,1,3,2,0:T(1,128)} %get-tuple-element.755) | copy-start | bytes 6148
  261.7 28.6 %copy-start.192 = (s32[1,16]{1,0:T(1,128)S(1)}, s32[1,16]{1,0:T(1,128)}, u32[]{:S(2)}) copy-start(s32[1,16]{1,0:T(1,128)} %param.13) | copy-start | bytes 196
  261.7 28.6 %copy-start.190 = (f32[16]{0:T(128)S(1)}, f32[16]{0:T(128)}, u32[]{:S(2)}) copy-start(f32[16]{0:T(128)} %param.12) | copy-start | bytes 196
  261.7 28.7 %copy-start.2 = (bf16[16,24,512]{2,0,1:T(8,128)(2,1)S(1)}, bf16[16,24,512]{2,0,1:T(8,128)(2,1)}, u32[]{:S(2)}) copy-start(bf16[16,24,512]{2,0,1:T(8,128)(2,1)} %copy-done.1) | copy-start | bytes 1179652
  (134 other events, 643.4 us)
Sparse Core Ops, SparseCore 0:
  290.4 155.7 all-gather.2
where the time goes:
time: 473 us; the launch traced here: 465 us
  waiting for transfers between devices  159 us (34%)
  local copies, waits for them, and re-layouts  127 us (27%)
  other arithmetic  90.5 us (19%)
  matrix products  35.3 us (7%)
  blocking collectives  27.3 us (6%)
  between operations  17.7 us (4%)
  starting transfers between devices  5.46 us (1%)
    all_gather x1, waiting for transfers between devices, body(): lax.all_gather(flat_fields, 'ta', axis=0, tiled=True)  154 us
    unnamed x442, local copies, waits for them, and re-layouts  57.1 us
    psum x1, blocking collectives, body(): meson = lax.psum(partial_value, 'sa').astype(jnp.bfloat16)  27.3 us
    dot_general x4, matrix products, meson_plane(): lax.dot_general(left_rows.reshape(-1, width), right_cols, (((1,), (1,)),...  24.1 us
    another operation x16, local copies, waits for them, and re-layouts, meson_plane(): jnp.stack([apply_gamma(vectors, k) for k in range(4)]).reshape(-1, width)  21.9 us
    another operation x24, other arithmetic, apply_gamma(): return jnp.stack(spin_rows, axis=2)  21.6 us
    unnamed x24, other arithmetic  17.7 us
    add x8, other arithmetic, body(): running[s][c][q] + ahead[s][c][q] - ahead_gamma[s][c][q] + behind[s][c][q]  15.2 us
  transfers between devices with their start and end apart: 5, of which 3 were waited for; matrix products, arithmetic and copies ran while one was open for 20% of the time, Pallas kernels for 0%

commit v1 on v0

v1 whole, which is shorter than its diff:
```python
import functools
import math

import jax
import jax.numpy as jnp
from jax import lax
from jax.experimental import pallas as pl
from jax.experimental.pallas import tpu as pltpu
from jax.sharding import PartitionSpec as P

NMODE = 16
NMOM = 16
LS = 16
ZL = 4
F32 = jnp.float32
BF16 = jnp.bfloat16
MESH = pl.DeviceIdType.MESH

hop_kappa = 0.125
gamma_source = ((3, 2, 1, 0), (3, 2, 1, 0), (2, 3, 0, 1), (2, 3, 0, 1))
gamma_factor = ((3, 3, 2, 2), (1, 0, 0, 1), (3, 2, 2, 3), (0, 0, 0, 0))
factor_parts = ((1, 0), (-1, 0), (0, 1), (0, -1))


def add_factor(base, value, code, sign):
    (br, bi), (vr, vi) = base, value
    re, im = factor_parts[code]
    re, im = re * sign, im * sign
    if re == 1:
        return br + vr, bi + vi
    if re == -1:
        return br - vr, bi - vi
    if im == 1:
        return br - vi, bi + vr
    return br + vi, bi - vr


def project(spin, d, sign):
    return [
        [
            add_factor(spin[s][c], spin[gamma_source[d][s]][c], gamma_factor[d][s], sign)
            for c in range(3)
        ]
        for s in range(2)
    ]


def load_spin(load):
    return [[(load(s * 3 + c), load(12 + s * 3 + c)) for c in range(3)] for s in range(4)]


def link_times(load, half, adjoint):
    out = [[None] * 3 for _ in range(2)]
    for a in range(3):
        for b in range(3):
            lr, li = (load(0, b, a), load(1, b, a)) if adjoint else (load(0, a, b), load(1, a, b))
            for s in range(2):
                hr, hi = half[s][b]
                if adjoint:
                    re, im = lr * hr + li * hi, lr * hi - li * hr
                else:
                    re, im = lr * hr - li * hi, lr * hi + li * hr
                old = out[s][a]
                out[s][a] = (re, im) if old is None else (old[0] + re, old[1] + im)
    return out


def add_hop(total, half, d, sign):
    for s in range(2):
        for c in range(3):
            total[s][c] = (total[s][c][0] + half[s][c][0], total[s][c][1] + half[s][c][1])
    for s in range(2, 4):
        for c in range(3):
            total[s][c] = add_factor(
                total[s][c], half[gamma_source[d][s]][c], gamma_factor[d][s], sign
            )
    return total


def map_half(half, f):
    return [[(f(half[s][c][0]), f(half[s][c][1])) for c in range(3)] for s in range(2)]


def halo_kernel(nt, ns, e_ref, e2_ref, ht_ref, hz_ref, ef, st, sz, ts_sem, tr_sem, zs_sem, zr_sem):
    t = lax.axis_index("ta")
    s = lax.axis_index("sa")
    t_up, t_dn = lax.rem(t + 1, nt), lax.rem(t + nt - 1, nt)
    s_up, s_dn = lax.rem(s + 1, ns), lax.rem(s + ns - 1, ns)
    partners = ((t_dn, s), (t_up, s), (t, s_dn), (t, s_up))
    barrier = pltpu.get_barrier_semaphore()
    for partner in partners:
        pl.semaphore_signal(barrier, inc=1, device_id=partner, device_id_type=MESH)

    def widen(m, carry):
        rows = pl.ds(pl.multiple_of(m * 96, 96), 96)
        ef[rows, :] = e_ref[rows, :].astype(F32)
        return carry

    lax.fori_loop(0, NMODE, widen, 0)
    sign_dn = jnp.where(t == 0, -1.0, 1.0).astype(F32)
    sign_up = jnp.where(t == nt - 1, -1.0, 1.0).astype(F32)
    copies = []
    for z in range(ZL):
        parts = []
        for g in range(2):
            parts.append(
                load_spin(
                    lambda comp: ef[pl.ds((g * 8 * 24 + comp) * 4 + z, 8, stride=96), :]
                )
            )
        both = [
            [
                tuple(
                    jnp.concatenate([parts[0][a][c][q], parts[1][a][c][q]], axis=0)
                    for q in range(2)
                )
                for c in range(3)
            ]
            for a in range(4)
        ]
        for a in range(4):
            for c in range(3):
                for q in range(2):
                    e2_ref[z, q * 12 + a * 3 + c] = both[a][c][q].astype(BF16)
        for way, sign, factor in ((0, -1, sign_dn), (1, 1, sign_up)):
            half = project(both, 3, sign)
            for a in range(2):
                for c in range(3):
                    for q in range(2):
                        st[way, z, q * 6 + a * 3 + c] = (half[a][c][q] * factor).astype(BF16)
        for edge, way, sign in ((0, 0, -1), (ZL - 1, 1, 1)):
            if z == edge:
                half = project(both, 2, sign)
                for a in range(2):
                    for c in range(3):
                        for q in range(2):
                            sz[way, q * 6 + a * 3 + c] = half[a][c][q].astype(BF16)
        if z == 0:
            pl.semaphore_wait(barrier, 4)
        for way in range(2):
            copy = pltpu.make_async_remote_copy(
                src_ref=st.at[way, z],
                dst_ref=ht_ref.at[way, z],
                send_sem=ts_sem.at[way, z],
                recv_sem=tr_sem.at[way, z],
                device_id=partners[way],
                device_id_type=MESH,
            )
            copy.start()
            copies.append(copy)
        for edge, way in ((0, 0), (ZL - 1, 1)):
            if z == edge:
                copy = pltpu.make_async_remote_copy(
                    src_ref=sz.at[way],
                    dst_ref=hz_ref.at[way],
                    send_sem=zs_sem.at[way],
                    recv_sem=zr_sem.at[way],
                    device_id=partners[2 + way],
                    device_id_type=MESH,
                )
                copy.start()
                copies.append(copy)
    for copy in copies:
        copy.wait()


def circle(step):
    fold = jnp.where(step > 8, 16 - step, step)
    low = jnp.where(fold > 4, 8 - fold, fold)
    value = jnp.where(low == 1, math.cos(math.pi / 8), 1.0).astype(F32)
    value = jnp.where(low == 2, math.cos(math.pi / 4), value).astype(F32)
    value = jnp.where(low == 3, math.cos(3 * math.pi / 8), value).astype(F32)
    value = jnp.where(low == 4, 0.0, value).astype(F32)
    return jnp.where(fold > 4, -value, value)


def phase_tables(t, s, momenta, cos_ref, sin_ref):
    lane = lax.broadcasted_iota(jnp.int32, (NMOM, 128), 1)
    y, h = lane >> 3, lane & 7
    nx, ny, nz = momenta[:, 0:1], momenta[:, 1:2], momenta[:, 2:3]
    for parity in range(2):
        for zl in range(ZL):
            z = s * ZL + zl
            x = 2 * h + ((t + z + y + parity) & 1)
            step = (nx * x + ny * y + nz * z) & 15
            cos_ref[parity, zl] = circle(step)
            sin_ref[parity, zl] = circle((step + 12) & 15)


def meson_part(modes_ref, parity, z, cos_ref, sin_ref, total_ref):
    for a in range(4):
        for c in range(3):
            comp = a * 3 + c
            vr = modes_ref[z, comp].astype(F32)
            vi = modes_ref[z, 12 + comp].astype(F32)
            rows = []
            for p in range(NMOM):
                cs = cos_ref[parity, z, pl.ds(p, 1), :]
                sn = sin_ref[parity, z, pl.ds(p, 1), :]
                rows.append(
                    jnp.concatenate(
                        [
                            (vr * cs - vi * sn).astype(BF16),
                            (-(vr * sn + vi * cs)).astype(BF16),
                        ],
                        axis=1,
                    )
                )
            left = jnp.concatenate(rows, axis=0)
            real_rows, imag_rows = [], []
            for k in range(4):
                other = gamma_source[k][a] * 3 + c
                wr = modes_ref[z, other]
                wi = modes_ref[z, 12 + other]
                re, im = factor_parts[gamma_factor[k][a]]
                if re == 1:
                    gr, gi = wr, wi
                elif re == -1:
                    gr, gi = -wr, -wi
                elif im == 1:
                    gr, gi = -wi, wr
                else:
                    gr, gi = wi, -wr
                real_rows.append(jnp.concatenate([gr, -gi], axis=1))
                imag_rows.append(jnp.concatenate([gi, gr], axis=1))
            right = jnp.concatenate(real_rows + imag_rows, axis=0)
            total_ref[...] += lax.dot_general(
                left, right, (((1,), (1,)), ((), ())), preferred_element_type=F32
            )


def field_kernel(
    e2_ref, ht_ref, hz_ref, links_ref, clover_ref, momenta_ref,
    odd_ref, total_ref,
    ef, tf, zf, lf, ob, of, cos_ref, sin_ref,
):
    t = lax.axis_index("ta")
    s = lax.axis_index("sa")
    phase_tables(t, s, momenta_ref[...], cos_ref, sin_ref)
    total_ref[...] = jnp.zeros_like(total_ref)

    def even_step(z, carry):
        meson_part(e2_ref, 0, z, cos_ref, sin_ref, total_ref)
        return carry

    lax.fori_loop(0, ZL, even_step, 0)

    def widen_links(i, carry):
        rows = pl.ds(pl.multiple_of(i * 96, 96), 96)
        lf[rows, :] = links_ref[rows, :].astype(F32)
        return carry

    lax.fori_loop(0, 6, widen_links, 0)

    def widen(z, carry):
        ef[z] = e2_ref[z].astype(F32)
        tf[0, z] = ht_ref[0, z].astype(F32)
        tf[1, z] = ht_ref[1, z].astype(F32)
        return carry

    lax.fori_loop(0, ZL, widen, 0)
    zf[0, ZL - 1] = hz_ref[0].astype(F32)
    zf[1, 0] = hz_ref[1].astype(F32)

    def z_halves(i, carry):
        z, g = i // 2, i % 2
        rows = pl.ds(pl.multiple_of(g * 8, 8), 8)
        for way, sign, source, target in ((0, -1, z + 1, z), (1, 1, z, z + 1)):
            half = project(load_spin(lambda comp: ef[source, comp, rows, :]), 2, sign)
            for a in range(2):
                for c in range(3):
                    for q in range(2):
                        zf[way, target, q * 6 + a * 3 + c, rows, :] = half[a][c][q]
        return carry

    lax.fori_loop(0, 2 * (ZL - 1), z_halves, 0)

    lane = lax.broadcasted_iota(jnp.int32, (8, 128), 1)
    first, last = (lane & 7) == 0, (lane & 7) == 7

    def hop_step(i, carry):
        z, g = i // 2, i % 2
        rows = pl.ds(pl.multiple_of(g * 8, 8), 8)
        shifted = ((t + s * ZL + z + (lane >> 3) + 1) & 1) == 1
        spin = load_spin(lambda comp: ef[z, comp, rows, :])
        zero = jnp.zeros((8, 128), F32)
        total = [[(zero, zero) for _ in range(3)] for _ in range(4)]

        def x_ahead(v):
            ahead = jnp.where(last, pltpu.roll(v, 7, 1), pltpu.roll(v, 127, 1))
            return jnp.where(shifted, ahead, v)

        def x_behind(v):
            behind = jnp.where(first, pltpu.roll(v, 121, 1), pltpu.roll(v, 1, 1))
            return jnp.where(shifted, v, behind)

        def link(way, d):
            def load(q, a, b):
                row = ((((way * 4 + d) * 2 + q) * 3 + a) * 3 + b) * ZL
                return lf[pl.ds(row + z, 1), :]

            return load

        def stored(ref, way):
            return [
                [(ref[way, z, a * 3 + c, rows, :], ref[way, z, 6 + a * 3 + c, rows, :]) for c in range(3)]
                for a in range(2)
            ]

        for way, sign in ((0, -1), (1, 1)):
            for d in range(4):
                if d == 0:
                    half = map_half(project(spin, 0, sign), (x_ahead, x_behind)[way])
                elif d == 1:
                    half = map_half(
                        project(spin, 1, sign), lambda v: pltpu.roll(v, (120, 8)[way], 1)
                    )
                else:
                    half = stored(zf if d == 2 else tf, way)
                total = add_hop(total, link_times(link(way, d), half, way == 1), d, sign)

        for chir in range(2):
            source = [
                tuple(hop_kappa * total[2 * chir + col // 3][col % 3][q] for q in range(2))
                for col in range(6)
            ]
            for r in range(6):
                out_real = out_imag = None
                for col in range(6):
                    row = ((chir * 2 * 6 + r) * 6 + col) * ZL
                    cr = clover_ref[pl.ds(row + z, 1), :]
                    ci = clover_ref[pl.ds(row + 36 * ZL + z, 1), :]
                    vr, vi = source[col]
                    re, im = cr * vr - ci * vi, cr * vi + ci * vr
                    out_real = re if out_real is None else out_real + re
                    out_imag = im if out_imag is None else out_imag + im
                place = 6 * chir + r
                for q, value in ((0, out_real), (12, out_imag)):
                    of[z, q + place, rows, :] = value
        return carry

    lax.fori_loop(0, 2 * ZL, hop_step, 0)

    def odd_step(z, carry):
        ob[z] = of[z].astype(BF16)
        meson_part(ob, 1, z, cos_ref, sin_ref, total_ref)
        return carry

    lax.fori_loop(0, ZL, odd_step, 0)
    turned = lf

    def turn(comp, carry):
        for z in range(ZL):
            for g in range(2):
                turned[pl.ds(g * 32 + z, 8, stride=4), :] = of[z, comp, pl.ds(g * 8, 8), :]
        odd_ref[:, comp] = turned[pl.ds(0, 64), :].astype(BF16).reshape(NMODE, ZL, 128)
        return carry

    lax.fori_loop(0, 24, turn, 0)


def pair_kernel(
    nt, ns, total_ref, weights_ref, sep_ref, out_ref,
    arrive, flat, rows_out, rows_in, gathered, gram, back, last,
    rs_send, rs_recv, a_send, a_recv, b_send, b_recv, l_send, l_recv,
):
    t = lax.axis_index("ta")
    s = lax.axis_index("sa")
    quarter = NMOM * NMODE // ns
    per = quarter // nt
    barrier = pltpu.get_barrier_semaphore()

    def greet(d, carry):
        pl.semaphore_signal(
            barrier, inc=1, device_id=(lax.rem(t + d, nt), s), device_id_type=MESH
        )
        return carry

    for d in range(1, ns):
        pl.semaphore_signal(
            barrier, inc=1, device_id=(t, lax.rem(s + d, ns)), device_id_type=MESH
        )
    lax.fori_loop(1, nt, greet, 0)
    pl.semaphore_wait(barrier, ns - 1 + nt - 1)

    copies = []
    for d in range(1, ns):
        partner = lax.rem(s + d, ns)
        copy = pltpu.make_async_remote_copy(
            src_ref=total_ref.at[pl.ds(pl.multiple_of(partner * quarter, quarter), quarter)],
            dst_ref=arrive.at[d - 1],
            send_sem=rs_send.at[d - 1],
            recv_sem=rs_recv.at[d - 1],
            device_id=(t, partner),
            device_id_type=MESH,
        )
        copy.start()
        copies.append(copy)
    mine = total_ref[pl.ds(pl.multiple_of(s * quarter, quarter), quarter), :]
    for d, copy in enumerate(copies):
        copy.wait()
        mine = mine + arrive[d]
    flat[pl.ds(0, quarter), :] = mine.astype(BF16).astype(F32)
    for o in range(nt):
        for r in range(per):
            rows_out[o, r] = flat[pl.ds(o * per + r, 1), :]

    def exchange(src, dst, send_sem, recv_sem):
        def send(d, carry):
            partner = lax.rem(t + d, nt)
            pltpu.make_async_remote_copy(
                src_ref=src.at[partner],
                dst_ref=dst.at[t],
                send_sem=send_sem,
                recv_sem=recv_sem,
                device_id=(partner, s),
                device_id_type=MESH,
            ).start()
            return carry

        lax.fori_loop(1, nt, send, 0)
        dst[pl.ds(t, 1)] = src[pl.ds(t, 1)]
        others = pl.ds(0, nt - 1)
        pltpu.make_async_copy(src.at[others], src.at[others], send_sem).wait()
        pltpu.make_async_copy(dst.at[others], dst.at[others], recv_sem).wait()

    exchange(rows_out, rows_in, a_send, a_recv)

    lane = lax.broadcasted_iota(jnp.int32, (NMODE, 128), 1)
    spread = (lane % NMODE == lax.broadcasted_iota(jnp.int32, (NMODE, 128), 0)).astype(F32)
    weights = weights_ref[...]
    weight_j = jnp.dot(weights, spread, precision=lax.Precision.HIGHEST, preferred_element_type=F32)
    mode = lax.broadcasted_iota(jnp.int32, (1, NMODE), 1)
    gathered[...] = jnp.zeros_like(gathered)
    product = None
    tall = max(nt, 8)
    for r in range(per):
        for k in range(nt):
            gathered[pl.ds(k, 1), :] = rows_in[k, r]
        weight_i = jnp.sum(
            jnp.where(mode == (t * per + r) % NMODE, weights, 0.0), axis=1, keepdims=True
        )
        everything = gathered[...]
        term = lax.dot_general(
            everything[:tall] * (weight_i * weight_j),
            everything,
            (((1,), (1,)), ((), ())),
            precision=lax.Precision.HIGHEST,
            preferred_element_type=F32,
        )
        product = term if product is None else product + term
    flat[pl.ds(0, tall), :] = product
    for k in range(nt):
        gram[k] = flat[pl.ds(k, 1), :]
    exchange(gram, back, b_send, b_recv)
    row = jnp.sum(back[...], axis=0)
    last[0] = row
    copies = []
    for d in range(1, ns):
        copy = pltpu.make_async_remote_copy(
            src_ref=last.at[0],
            dst_ref=last.at[d],
            send_sem=l_send.at[d - 1],
            recv_sem=l_recv.at[d - 1],
            device_id=(t, lax.rem(s + d, ns)),
            device_id_type=MESH,
        )
        copy.start()
        copies.append(copy)
    for d, copy in enumerate(copies):
        copy.wait()
        row = row + last[d + 1]
    sink = lax.rem(t + sep_ref[...], nt)
    chosen = (lax.broadcasted_iota(jnp.int32, (128, 16), 0) == sink).astype(F32)
    picked = jnp.dot(row, chosen, precision=lax.Precision.HIGHEST, preferred_element_type=F32)
    out_ref[...] = picked * (1.0 / (16.0 * NMODE * NMOM * LS**3))


def body(nt, ns, even_modes, hop_links, clover_inverse, momenta, mode_weights, separations):
    vmem = pl.BlockSpec(memory_space=pltpu.VMEM)
    limit = 48 * 1024 * 1024
    shape = jax.ShapeDtypeStruct
    dma = pltpu.SemaphoreType.DMA
    e2, ht, hz = pl.pallas_call(
        functools.partial(halo_kernel, nt, ns),
        out_shape=(
            shape((ZL, 24, NMODE, 128), BF16),
            shape((2, ZL, 12, NMODE, 128), BF16),
            shape((2, 12, NMODE, 128), BF16),
        ),
        in_specs=[vmem],
        out_specs=(vmem, vmem, vmem),
        scratch_shapes=[
            pltpu.VMEM((NMODE * 24 * ZL, 128), F32),
            pltpu.VMEM((2, ZL, 12, NMODE, 128), BF16),
            pltpu.VMEM((2, 12, NMODE, 128), BF16),
            dma((2, ZL)), dma((2, ZL)), dma((2,)), dma((2,)),
        ],
        compiler_params=pltpu.CompilerParams(
            collective_id=0, has_side_effects=True, vmem_limit_bytes=limit
        ),
        name="halo",
    )(even_modes.reshape(NMODE * 24 * ZL, 128))
    odd_modes, total = pl.pallas_call(
        field_kernel,
        out_shape=(
            shape((NMODE, 24, ZL, 128), BF16),
            shape((NMOM * NMODE, 128), F32),
        ),
        in_specs=[vmem] * 6,
        out_specs=(vmem, vmem),
        scratch_shapes=[
            pltpu.VMEM((ZL, 24, NMODE, 128), F32),
            pltpu.VMEM((2, ZL, 12, NMODE, 128), F32),
            pltpu.VMEM((2, ZL, 12, NMODE, 128), F32),
            pltpu.VMEM((144 * ZL, 128), F32),
            pltpu.VMEM((ZL, 24, NMODE, 128), BF16),
            pltpu.VMEM((ZL, 24, NMODE, 128), F32),
            pltpu.VMEM((2, ZL, NMOM, 128), F32),
            pltpu.VMEM((2, ZL, NMOM, 128), F32),
        ],
        compiler_params=pltpu.CompilerParams(vmem_limit_bytes=limit),
        name="fields",
    )(e2, ht, hz, hop_links.reshape(144 * ZL, 128), clover_inverse.reshape(144 * ZL, 128), momenta)
    quarter = NMOM * NMODE // ns
    per = quarter // nt
    correlator = pl.pallas_call(
        functools.partial(pair_kernel, nt, ns),
        out_shape=shape((1, 16), F32),
        in_specs=[vmem] * 3,
        out_specs=vmem,
        scratch_shapes=[
            pltpu.VMEM((ns - 1, quarter, 128), F32),
            pltpu.VMEM((max(quarter, nt), 128), F32),
            pltpu.VMEM((nt, per, 1, 128), F32),
            pltpu.VMEM((nt, per, 1, 128), F32),
            pltpu.VMEM((128, 128), F32),
            pltpu.VMEM((nt, 1, 128), F32),
            pltpu.VMEM((nt, 1, 128), F32),
            pltpu.VMEM((ns, 1, 128), F32),
            dma((ns - 1,)), dma((ns - 1,)), dma, dma, dma, dma, dma((ns - 1,)), dma((ns - 1,)),
        ],
        compiler_params=pltpu.CompilerParams(
            collective_id=1, has_side_effects=True, vmem_limit_bytes=limit
        ),
        name="pairs",
    )(total, mode_weights.reshape(1, NMODE), separations)
    return odd_modes.reshape(even_modes.shape), correlator


def solution(mesh):
    in_specs = (
        P(None, None, None, None, "ta", "sa", None),
        P(None, None, None, None, None, "ta", "sa", None),
        P(None, None, None, None, "ta", "sa", None),
        P(),
        P(),
        P("ta", None),
    )
    out_specs = (P(None, None, None, None, "ta", "sa", None), P("ta", None))
    return jax.shard_map(
        functools.partial(body, mesh.shape["ta"], mesh.shape["sa"]),
        mesh=mesh,
        in_specs=in_specs,
        out_specs=out_specs,
        check_vma=False,
    )
```

time: 473 us -> 61.7 us (0.13)
  the two profiles are of different devices: /device:TPU:8 before, /device:TPU:1 now
where the time goes in v1:
time: 61.7 us; the launch traced here: 61.5 us
  Pallas kernels  57 us (92%)
  local copies, waits for them, and re-layouts  3.84 us (6%)
  between operations  0.67 us (1%)
    pallas_call x1, Pallas kernels, body(): pl.pallas_call(functools.partial(pair_kernel, nt, ns), out_shape=shape((1...  29.8 us
    pallas_call x1, Pallas kernels, body(): pl.pallas_call(functools.partial(halo_kernel, nt, ns), out_shape=(shape((...  18.4 us
    pallas_call x1, Pallas kernels, body(): pl.pallas_call(field_kernel, out_shape=(shape((NMODE, 24, ZL, 128), BF16)...  8.8 us
    unnamed x14, local copies, waits for them, and re-layouts  3.84 us

profile of v1, /device:TPU:1, one launch (start us, length us, event | category | flops | bytes accessed | tf_op | source)
XLA Modules:
  0.0 61.5 jit_solution(17073366314383121454)
XLA Ops:
  0.6 0.0 copy-start.5
  0.6 0.7 %copy-done.5 = s32[16,3]{0,1:T(4,128)S(1)} copy-done((s32[16,3]{0,1:T(4,128)S(1)}, s32[16,3]{0,1:T(4,128)}, u32[]{:S(2)}) %copy-start.5) | copy-done | bytes 216
  1.3 0.1 copy.8.momenta_ref
  1.4 0.0 copy-start
  1.4 1.0 %copy-done = bf16[16,2,4,3,1,4,128]{6,5,4,3,2,1,0:T(4,128)(2,1)S(1)} copy-done((bf16[16,2,4,3,1,4,128]{6,5,4,3,2,1,0:T(4,128)(2,1)S(1)}, bf16[16,2,4,3,1,4,128]{6,5,4,3,2,1,0:T(4,128)(2,1)}, u32[]{:S(2)}) %copy-start) | copy-done | bytes 393240
  2.4 0.0 copy-start.1
  2.4 18.4 %halo.1 = (bf16[4,24,16,128]{3,2,1,0:T(8,128)(2,1)S(1)}, bf16[2,4,12,16,128]{4,3,2,1,0:T(8,128)(2,1)S(1)}, bf16[2,12,16,128]{3,2,1,0:T(8,128)(2,1)S(1)}) custom-call(bf16[1536,128]{1,0:T(8,128)(2,1)S(1)} %bitcast.7), custom_call_target="tpu_custom_call" | custom-call | tf_op jit(solution)/shard_map/halo/pallas_call | solution.py:484
  20.8 0.0 copy-done.1
  20.8 0.0 copy-start.2
  20.8 0.9 %copy-done.2 = bf16[2,4,2,3,3,1,4,128]{7,6,5,4,3,2,1,0:T(4,128)(2,1)S(1)} copy-done((bf16[2,4,2,3,3,1,4,128]{7,6,5,4,3,2,1,0:T(4,128)(2,1)S(1)}, bf16[2,4,2,3,3,1,4,128]{7,6,5,4,3,2,1,0:T(4,128)(2,1)}, u32[]{:S(2)}) %copy-start.2) | copy-done | bytes 147480
  21.7 8.8 %fields.1 = (bf16[16,24,4,128]{3,2,1,0:T(4,128)(2,1)}, f32[256,128]{1,0:T(8,128)S(1)}) custom-call(bf16[4,24,16,128]{3,2,1,0:T(8,128)(2,1)S(1)} %get-tuple-element.7.e2_ref, bf16[2,4,12,16,128]{4,3,2,1,0:T(8,128)(2,1)S(1)} %get-tuple-element.8.ht_ref, bf16[2,12,16,128]{3,2,1,0:T(8,128)(2,1)S(1)} %get-tuple-element.9.hz_ref, bf16[576,128]{1,0:T(8,128)(2,1)S(1)} %bitcast.9, ...), custom_call_target="tpu_custom_call" | custom-call | tf_op jit(solution)/shard_map/fields/pallas_call | solution.py:504
  30.5 0.0 copy-start.3
  30.5 0.0 copy-start.4
  30.5 0.7 %copy-done.3 = f32[16]{0:T(128)S(1)} copy-done((f32[16]{0:T(128)S(1)}, f32[16]{0:T(128)}, u32[]{:S(2)}) %copy-start.3) | copy-done | bytes 88
  31.2 0.0 copy-done.4
  31.2 29.8 %pairs.1 = f32[1,16]{1,0:T(1,128)S(1)} custom-call(f32[256,128]{1,0:T(8,128)S(1)} %get-tuple-element.11.total_ref, f32[1,16]{1,0:T(1,128)S(1)} %bitcast.10, s32[1,16]{1,0:T(1,128)S(1)} %copy-done.4), custom_call_target="tpu_custom_call" | custom-call | tf_op jit(solution)/shard_map/pairs/pallas_call | solution.py:527
  61.0 0.5 copy.11
Async XLA Ops:
  0.6 0.7 %copy-start.5 = (s32[16,3]{0,1:T(4,128)S(1)}, s32[16,3]{0,1:T(4,128)}, u32[]{:S(2)}) copy-start(s32[16,3]{0,1:T(4,128)} %param.9) | copy-start | bytes 580
  1.4 1.0 %copy-start = (bf16[16,2,4,3,1,4,128]{6,5,4,3,2,1,0:T(4,128)(2,1)S(1)}, bf16[16,2,4,3,1,4,128]{6,5,4,3,2,1,0:T(4,128)(2,1)}, u32[]{:S(2)}) copy-start(bf16[16,2,4,3,1,4,128]{6,5,4,3,2,1,0:T(4,128)(2,1)} %param.6) | copy-start | bytes 1179652
  2.4 18.4 %copy-start.1 = (f32[2,2,6,6,1,4,128]{6,5,4,3,2,1,0:T(4,128)S(1)}, f32[2,2,6,6,1,4,128]{6,5,4,3,2,1,0:T(4,128)}, u32[]{:S(2)}) copy-start(f32[2,2,6,6,1,4,128]{6,5,4,3,2,1,0:T(4,128)} %param.8) | copy-start | bytes 884740
  20.8 0.9 %copy-start.2 = (bf16[2,4,2,3,3,1,4,128]{7,6,5,4,3,2,1,0:T(4,128)(2,1)S(1)}, bf16[2,4,2,3,3,1,4,128]{7,6,5,4,3,2,1,0:T(4,128)(2,1)}, u32[]{:S(2)}) copy-start(bf16[2,4,2,3,3,1,4,128]{7,6,5,4,3,2,1,0:T(4,128)(2,1)} %param.7) | copy-start | bytes 442372
  30.5 0.7 %copy-start.3 = (f32[16]{0:T(128)S(1)}, f32[16]{0:T(128)}, u32[]{:S(2)}) copy-start(f32[16]{0:T(128)} %param.10) | copy-start | bytes 196
  30.5 0.7 %copy-start.4 = (s32[1,16]{1,0:T(1,128)S(1)}, s32[1,16]{1,0:T(1,128)}, u32[]{:S(2)}) copy-start(s32[1,16]{1,0:T(1,128)} %sep_ref.1) | copy-start | bytes 196

commit v2 on v1

v2 whole, which is shorter than its diff:
```python
import functools
import math

import jax
import jax.numpy as jnp
from jax import lax
from jax.experimental import pallas as pl
from jax.experimental.pallas import tpu as pltpu
from jax.sharding import PartitionSpec as P

NMODE = 16
NMOM = 16
LS = 16
ZL = 4
F32 = jnp.float32
BF16 = jnp.bfloat16
MESH = pl.DeviceIdType.MESH

hop_kappa = 0.125
gamma_source = ((3, 2, 1, 0), (3, 2, 1, 0), (2, 3, 0, 1), (2, 3, 0, 1))
gamma_factor = ((3, 3, 2, 2), (1, 0, 0, 1), (3, 2, 2, 3), (0, 0, 0, 0))
factor_parts = ((1, 0), (-1, 0), (0, 1), (0, -1))


def add_factor(base, value, code, sign):
    (br, bi), (vr, vi) = base, value
    re, im = factor_parts[code]
    re, im = re * sign, im * sign
    if re == 1:
        return br + vr, bi + vi
    if re == -1:
        return br - vr, bi - vi
    if im == 1:
        return br - vi, bi + vr
    return br + vi, bi - vr


def project(spin, d, sign):
    return [
        [
            add_factor(spin[s][c], spin[gamma_source[d][s]][c], gamma_factor[d][s], sign)
            for c in range(3)
        ]
        for s in range(2)
    ]


def load_spin(load):
    return [[(load(s * 3 + c), load(12 + s * 3 + c)) for c in range(3)] for s in range(4)]


def link_times(load, half, adjoint):
    out = [[None] * 3 for _ in range(2)]
    for a in range(3):
        for b in range(3):
            lr, li = (load(0, b, a), load(1, b, a)) if adjoint else (load(0, a, b), load(1, a, b))
            for s in range(2):
                hr, hi = half[s][b]
                if adjoint:
                    re, im = lr * hr + li * hi, lr * hi - li * hr
                else:
                    re, im = lr * hr - li * hi, lr * hi + li * hr
                old = out[s][a]
                out[s][a] = (re, im) if old is None else (old[0] + re, old[1] + im)
    return out


def add_hop(total, half, d, sign):
    for s in range(2):
        for c in range(3):
            total[s][c] = (total[s][c][0] + half[s][c][0], total[s][c][1] + half[s][c][1])
    for s in range(2, 4):
        for c in range(3):
            total[s][c] = add_factor(
                total[s][c], half[gamma_source[d][s]][c], gamma_factor[d][s], sign
            )
    return total


def map_half(half, f):
    return [[(f(half[s][c][0]), f(half[s][c][1])) for c in range(3)] for s in range(2)]


def circle(step):
    fold = jnp.where(step > 8, 16 - step, step)
    low = jnp.where(fold > 4, 8 - fold, fold)
    value = jnp.where(low == 1, math.cos(math.pi / 8), 1.0).astype(F32)
    value = jnp.where(low == 2, math.cos(math.pi / 4), value).astype(F32)
    value = jnp.where(low == 3, math.cos(3 * math.pi / 8), value).astype(F32)
    value = jnp.where(low == 4, 0.0, value).astype(F32)
    return jnp.where(fold > 4, -value, value)


def phase_tables(t, s, momenta, cos_ref, sin_ref):
    lane = lax.broadcasted_iota(jnp.int32, (NMOM, 128), 1)
    y, h = lane >> 3, lane & 7
    place = lax.broadcasted_iota(jnp.int32, (NMOM, NMOM), 1)
    diagonal = place == lax.broadcasted_iota(jnp.int32, (NMOM, NMOM), 0)
    nx, ny, nz = (
        jnp.sum(
            jnp.where(diagonal, momenta[d : d + 1, :].astype(F32), 0.0), axis=1, keepdims=True
        ).astype(jnp.int32)
        for d in range(3)
    )
    for parity in range(2):
        for zl in range(ZL):
            z = s * ZL + zl
            x = 2 * h + ((t + z + y + parity) & 1)
            step = (nx * x + ny * y + nz * z) & 15
            cos_ref[parity, zl] = circle(step)
            sin_ref[parity, zl] = circle((step + 12) & 15)


def meson_part(modes_ref, parity, z, cos_ref, sin_ref, total_ref):
    for a in range(4):
        for c in range(3):
            comp = a * 3 + c
            vr = modes_ref[z, comp].astype(F32)
            vi = modes_ref[z, 12 + comp].astype(F32)
            rows = []
            for p in range(NMOM):
                cs = cos_ref[parity, z, pl.ds(p, 1), :]
                sn = sin_ref[parity, z, pl.ds(p, 1), :]
                rows.append(
                    jnp.concatenate(
                        [
                            (vr * cs - vi * sn).astype(BF16),
                            (-(vr * sn + vi * cs)).astype(BF16),
                        ],
                        axis=1,
                    )
                )
            left = jnp.concatenate(rows, axis=0)
            real_rows, imag_rows = [], []
            for k in range(4):
                other = gamma_source[k][a] * 3 + c
                wr = modes_ref[z, other]
                wi = modes_ref[z, 12 + other]
                re, im = factor_parts[gamma_factor[k][a]]
                if re == 1:
                    gr, gi = wr, wi
                elif re == -1:
                    gr, gi = -wr, -wi
                elif im == 1:
                    gr, gi = -wi, wr
                else:
                    gr, gi = wi, -wr
                real_rows.append(jnp.concatenate([gr, -gi], axis=1))
                imag_rows.append(jnp.concatenate([gi, gr], axis=1))
            right = jnp.concatenate(real_rows + imag_rows, axis=0)
            total_ref[...] += lax.dot_general(
                left, right, (((1,), (1,)), ((), ())), preferred_element_type=F32
            )


def kernel(
    nt, ns,
    e_hbm, links_hbm, clover_hbm, momenta_hbm, weights_hbm, sep_hbm,
    odd_ref, out_ref,
    e_ref, links_ref, clover_ref, momenta_ref, weights_ref, sep_ref,
    ef, ewide, e2, st, sz, ht, hz, tf, zf, lf, of, ob, cos_ref, sin_ref,
    total_ref, arr1, turn2, send2, arr2, gathered, send3, arr3, send4, arr4,
    in_sem, ts_sem, tr_sem, zs_sem, zr_sem, x_send, x_recv,
):
    t = lax.axis_index("ta")
    s = lax.axis_index("sa")
    tz, ty, tx = t // 8, lax.rem(t, 8) // 2, lax.rem(t, 2)
    t_up, t_dn = lax.rem(t + 1, nt), lax.rem(t + nt - 1, nt)
    s_up, s_dn = lax.rem(s + 1, ns), lax.rem(s + ns - 1, ns)
    partners = ((t_dn, s), (t_up, s), (t, s_dn), (t, s_up))
    mine_a = ty * 4 + s
    mine_b = tz * 2 + tx

    def member_a(index):
        return tz * 8 + (index // 4) * 2 + tx, lax.rem(index, 4)

    def member_b(index):
        return (index // 2) * 8 + ty * 2 + lax.rem(index, 2), s

    groups = ((mine_a, member_a), (mine_b, member_b))
    loads = []
    for i, (source, target) in enumerate(
        (
            (e_hbm, e_ref), (momenta_hbm, momenta_ref), (links_hbm, links_ref),
            (clover_hbm, clover_ref), (weights_hbm, weights_ref), (sep_hbm, sep_ref),
        )
    ):
        load = pltpu.make_async_copy(source, target, in_sem.at[i])
        load.start()
        loads.append(load)
    barrier = pltpu.get_barrier_semaphore()
    for partner in partners[:2]:
        pl.semaphore_signal(barrier, inc=1, device_id=partner, device_id_type=MESH)
    for mine, member in groups:
        def greet(d, carry, mine=mine, member=member):
            pl.semaphore_signal(
                barrier, inc=1, device_id=member(lax.rem(mine + d, 16)), device_id_type=MESH
            )
            return carry

        lax.fori_loop(1, 16, greet, 0)

    loads[0].wait()

    def widen(m, carry):
        rows = pl.ds(pl.multiple_of(m * 96, 96), 96)
        ewide[rows, :] = e_ref[rows, :].astype(F32)
        return carry

    lax.fori_loop(0, NMODE, widen, 0)
    sign_dn = jnp.where(t == 0, -1.0, 1.0).astype(F32)
    sign_up = jnp.where(t == nt - 1, -1.0, 1.0).astype(F32)

    def t_copy(way, z):
        return pltpu.make_async_remote_copy(
            src_ref=st.at[way, z],
            dst_ref=ht.at[way, z],
            send_sem=ts_sem.at[way, z],
            recv_sem=tr_sem.at[way, z],
            device_id=partners[way],
            device_id_type=MESH,
        )

    def z_copy(way):
        return pltpu.make_async_remote_copy(
            src_ref=sz.at[way],
            dst_ref=hz.at[way],
            send_sem=zs_sem.at[way],
            recv_sem=zr_sem.at[way],
            device_id=partners[2 + way],
            device_id_type=MESH,
        )

    def prepare(z):
        halves = []
        for g in range(2):
            halves.append(
                load_spin(
                    lambda comp: ewide[pl.ds((g * 8 * 24 + comp) * 4 + z, 8, stride=96), :]
                )
            )
        both = [
            [
                tuple(
                    jnp.concatenate([halves[0][a][c][q], halves[1][a][c][q]], axis=0)
                    for q in range(2)
                )
                for c in range(3)
            ]
            for a in range(4)
        ]
        for way, sign, factor in ((0, -1, sign_dn), (1, 1, sign_up)):
            half = project(both, 3, sign)
            for a in range(2):
                for c in range(3):
                    for q in range(2):
                        st[way, z, q * 6 + a * 3 + c] = (half[a][c][q] * factor).astype(BF16)
        for edge, way, sign in ((0, 0, -1), (ZL - 1, 1, 1)):
            if z == edge:
                half = project(both, 2, sign)
                for a in range(2):
                    for c in range(3):
                        for q in range(2):
                            sz[way, q * 6 + a * 3 + c] = half[a][c][q].astype(BF16)
        for a in range(4):
            for c in range(3):
                for q in range(2):
                    ef[z, q * 12 + a * 3 + c] = both[a][c][q]
                    e2[z, q * 12 + a * 3 + c] = both[a][c][q].astype(BF16)

    for z in range(ZL):
        prepare(z)
        if z == 0:
            pl.semaphore_wait(barrier, 32)
            z_copy(0).start()
        for way in range(2):
            t_copy(way, z).start()
    z_copy(1).start()

    loads[1].wait()
    phase_tables(t, s, momenta_ref[...], cos_ref, sin_ref)
    total_ref[...] = jnp.zeros_like(total_ref)

    def even_step(z, carry):
        meson_part(e2, 0, z, cos_ref, sin_ref, total_ref)
        return carry

    lax.fori_loop(0, ZL, even_step, 0)
    loads[2].wait()

    def widen_links(i, carry):
        rows = pl.ds(pl.multiple_of(i * 96, 96), 96)
        lf[rows, :] = links_ref[rows, :].astype(F32)
        return carry

    lax.fori_loop(0, 6, widen_links, 0)

    def z_halves(i, carry):
        z, g = i // 2, lax.rem(i, 2)
        rows = pl.ds(pl.multiple_of(g * 8, 8), 8)
        for way, sign, source, target in ((0, -1, z + 1, z), (1, 1, z, z + 1)):
            half = project(load_spin(lambda comp: ef[source, comp, rows, :]), 2, sign)
            for a in range(2):
                for c in range(3):
                    for q in range(2):
                        zf[way, target, q * 6 + a * 3 + c, rows, :] = half[a][c][q]
        return carry

    lax.fori_loop(0, 2 * (ZL - 1), z_halves, 0)
    for way in range(2):
        z_copy(way).wait_recv()
    zf[0, ZL - 1] = hz[0].astype(F32)
    zf[1, 0] = hz[1].astype(F32)
    lane = lax.broadcasted_iota(jnp.int32, (8, 128), 1)
    first, last = (lane & 7) == 0, (lane & 7) == 7

    def link(way, d, z):
        def load(q, a, b):
            row = ((((way * 4 + d) * 2 + q) * 3 + a) * 3 + b) * ZL
            return lf[pl.ds(row + z, 1), :]

        return load

    def stored(read):
        return [[(read(a * 3 + c), read(6 + a * 3 + c)) for c in range(3)] for a in range(2)]

    def near_step(i, carry):
        z, g = i // 2, lax.rem(i, 2)
        rows = pl.ds(pl.multiple_of(g * 8, 8), 8)
        shifted = ((t + s * ZL + z + (lane >> 3) + 1) & 1) == 1
        spin = load_spin(lambda comp: ef[z, comp, rows, :])
        zero = jnp.zeros((8, 128), F32)
        total = [[(zero, zero) for _ in range(3)] for _ in range(4)]

        def x_ahead(v):
            ahead = jnp.where(last, pltpu.roll(v, 7, 1), pltpu.roll(v, 127, 1))
            return jnp.where(shifted, ahead, v)

        def x_behind(v):
            behind = jnp.where(first, pltpu.roll(v, 121, 1), pltpu.roll(v, 1, 1))
            return jnp.where(shifted, v, behind)

        for way, sign in ((0, -1), (1, 1)):
            for d in range(3):
                if d == 0:
                    half = map_half(project(spin, 0, sign), (x_ahead, x_behind)[way])
                elif d == 1:
                    half = map_half(
                        project(spin, 1, sign), lambda v: pltpu.roll(v, (120, 8)[way], 1)
                    )
                else:
                    half = stored(lambda comp: zf[way, z, comp, rows, :])
                total = add_hop(total, link_times(link(way, d, z), half, way == 1), d, sign)
        for a in range(4):
            for c in range(3):
                for q in range(2):
                    of[z, q * 12 + a * 3 + c, rows, :] = total[a][c][q]
        return carry

    lax.fori_loop(0, 2 * ZL, near_step, 0)
    loads[3].wait()

    def far_step(z, carry):
        for way in range(2):
            t_copy(way, z).wait_recv()
            tf[way] = ht[way, z].astype(F32)

        def group_step(g, carry):
            rows = pl.ds(pl.multiple_of(g * 8, 8), 8)
            total = load_spin(lambda comp: of[z, comp, rows, :])
            for way, sign in ((0, -1), (1, 1)):
                half = stored(lambda comp: tf[way, comp, rows, :])
                total = add_hop(total, link_times(link(way, 3, z), half, way == 1), 3, sign)
            for chir in range(2):
                source = [
                    tuple(hop_kappa * total[2 * chir + col // 3][col % 3][q] for q in range(2))
                    for col in range(6)
                ]
                for r in range(6):
                    out_real = out_imag = None
                    for col in range(6):
                        row = ((chir * 2 * 6 + r) * 6 + col) * ZL
                        cr = clover_ref[pl.ds(row + z, 1), :]
                        ci = clover_ref[pl.ds(row + 36 * ZL + z, 1), :]
                        vr, vi = source[col]
                        re, im = cr * vr - ci * vi, cr * vi + ci * vr
                        out_real = re if out_real is None else out_real + re
                        out_imag = im if out_imag is None else out_imag + im
                    place = 6 * chir + r
                    of[z, place, rows, :] = out_real
                    of[z, 12 + place, rows, :] = out_imag
            return carry

        lax.fori_loop(0, 2, group_step, 0)
        ob[z] = of[z].astype(BF16)
        meson_part(ob, 1, z, cos_ref, sin_ref, total_ref)
        return carry

    lax.fori_loop(0, ZL, far_step, 0)

    def send(stage, group, source, target):
        mine, member = group

        def one(d, carry):
            other = lax.rem(mine + d, 16)
            pltpu.make_async_remote_copy(
                src_ref=source(other),
                dst_ref=target.at[mine],
                send_sem=x_send.at[stage],
                recv_sem=x_recv.at[stage],
                device_id=member(other),
                device_id_type=MESH,
            ).start()
            return carry

        lax.fori_loop(1, 16, one, 0)

    def wait(stage, target, sems):
        others = target.at[pl.ds(0, 15)]
        pltpu.make_async_copy(others, others, sems.at[stage]).wait()

    def rows_a(index):
        return pl.ds(pl.multiple_of(index * 16, 16), 16)

    send(0, groups[0], lambda i: total_ref.at[rows_a(i)], arr1)
    arr1[mine_a] = total_ref[rows_a(mine_a), :]

    def turn(comp, carry):
        for z in range(ZL):
            for g in range(2):
                lf[pl.ds(g * 32 + z, 8, stride=4), :] = of[z, comp, pl.ds(g * 8, 8), :]
        odd_ref[:, comp] = lf[pl.ds(0, 64), :].astype(BF16).reshape(NMODE, ZL, 128)
        return carry

    lax.fori_loop(0, 24, turn, 0)
    loads[4].wait()
    loads[5].wait()
    wait(0, arr1, x_recv)
    for y in range(4):
        field = arr1[4 * y] + arr1[4 * y + 1] + arr1[4 * y + 2] + arr1[4 * y + 3]
        field = field.astype(BF16).astype(F32)
        for g in range(2):
            turn2[pl.ds(g * 32 + y, 8, stride=4), :] = field[g * 8 : g * 8 + 8]
    for i in range(16):
        send2[i] = turn2[pl.ds(i * 4, 4), :]
    send(1, groups[1], lambda i: send2.at[i], arr2)
    arr2[mine_b] = send2[mine_b]
    weights = weights_ref[...]
    lane16 = lax.broadcasted_iota(jnp.int32, (NMODE, 128), 1)
    spread = (lane16 % NMODE == lax.broadcasted_iota(jnp.int32, (NMODE, 128), 0)).astype(F32)
    weight_j = jnp.dot(weights, spread, precision=lax.Precision.HIGHEST, preferred_element_type=F32)
    mode = lax.broadcasted_iota(jnp.int32, (1, NMODE), 1)
    weight_i = jnp.sum(jnp.where(mode == mine_b, weights, 0.0), axis=1, keepdims=True)
    pair_weight = weight_i * weight_j
    gathered[...] = jnp.zeros_like(gathered)
    wait(1, arr2, x_recv)
    for i in range(16):
        gathered[pl.ds(i * 4, 4), :] = arr2[i]
    everything = gathered[...]
    product = lax.dot_general(
        everything[:64] * pair_weight,
        everything,
        (((1,), (1,)), ((), ())),
        precision=lax.Precision.HIGHEST,
        preferred_element_type=F32,
    )
    turn2[...] = product
    for i in range(16):
        send3[i] = turn2[pl.ds(i * 4, 4), :]
    send(2, groups[1], lambda i: send3.at[i], arr3)
    arr3[mine_b] = send3[mine_b]
    wait(2, arr3, x_recv)
    part = jnp.sum(arr3[...], axis=0)
    for y in range(4):
        send4[y] = part[y : y + 1]
    send(3, groups[0], lambda i: send4.at[i // 4], arr4)
    arr4[mine_a] = send4[ty]
    sink = lax.rem(t + sep_ref[...], nt)
    column = (sink // 8 * 2 + lax.rem(sink, 2)) * 4 + lax.rem(sink, 8) // 2
    chosen = (lax.broadcasted_iota(jnp.int32, (128, 16), 0) == column).astype(F32)
    wait(3, arr4, x_recv)
    row = jnp.sum(arr4[...], axis=0)
    picked = jnp.dot(row, chosen, precision=lax.Precision.HIGHEST, preferred_element_type=F32)
    out_ref[...] = picked * (1.0 / (16.0 * NMODE * NMOM * LS**3))
    for way in range(2):
        z_copy(way).wait_send()
        for z in range(ZL):
            t_copy(way, z).wait_send()
    for stage, target in enumerate((arr1, arr2, arr3, arr4)):
        wait(stage, target, x_send)


def body(nt, ns, even_modes, hop_links, clover_inverse, momenta, mode_weights, separations):
    vmem = pl.BlockSpec(memory_space=pltpu.VMEM)
    hbm = pl.BlockSpec(memory_space=pltpu.HBM)
    shape = jax.ShapeDtypeStruct
    dma = pltpu.SemaphoreType.DMA
    sites = (ZL, 24, NMODE, 128)
    odd_modes, correlator = pl.pallas_call(
        functools.partial(kernel, nt, ns),
        out_shape=(shape((NMODE, 24, ZL, 128), BF16), shape((1, 16), F32)),
        in_specs=[hbm] * 6,
        out_specs=(vmem, vmem),
        scratch_shapes=[
            pltpu.VMEM((NMODE * 24 * ZL, 128), BF16),
            pltpu.VMEM((144 * ZL, 128), BF16),
            pltpu.VMEM((144 * ZL, 128), F32),
            pltpu.VMEM((3, NMOM), jnp.int32),
            pltpu.VMEM((1, NMODE), F32),
            pltpu.VMEM((1, 16), jnp.int32),
            pltpu.VMEM(sites, F32),
            pltpu.VMEM((NMODE * 24 * ZL, 128), F32),
            pltpu.VMEM(sites, BF16),
            pltpu.VMEM((2, ZL, 12, NMODE, 128), BF16),
            pltpu.VMEM((2, 12, NMODE, 128), BF16),
            pltpu.VMEM((2, ZL, 12, NMODE, 128), BF16),
            pltpu.VMEM((2, 12, NMODE, 128), BF16),
            pltpu.VMEM((2, 12, NMODE, 128), F32),
            pltpu.VMEM((2, ZL, 12, NMODE, 128), F32),
            pltpu.VMEM((144 * ZL, 128), F32),
            pltpu.VMEM(sites, F32),
            pltpu.VMEM(sites, BF16),
            pltpu.VMEM((2, ZL, NMOM, 128), F32),
            pltpu.VMEM((2, ZL, NMOM, 128), F32),
            pltpu.VMEM((NMOM * NMODE, 128), F32),
            pltpu.VMEM((16, 16, 128), F32),
            pltpu.VMEM((64, 128), F32),
            pltpu.VMEM((16, 4, 128), F32),
            pltpu.VMEM((16, 4, 128), F32),
            pltpu.VMEM((128, 128), F32),
            pltpu.VMEM((16, 4, 128), F32),
            pltpu.VMEM((16, 4, 128), F32),
            pltpu.VMEM((4, 1, 128), F32),
            pltpu.VMEM((16, 1, 128), F32),
            dma((6,)), dma((2, ZL)), dma((2, ZL)), dma((2,)), dma((2,)), dma((4,)), dma((4,)),
        ],
        compiler_params=pltpu.CompilerParams(
            collective_id=0, has_side_effects=True, vmem_limit_bytes=63 * 1024 * 1024
        ),
        name="correlator",
    )(
        even_modes.reshape(NMODE * 24 * ZL, 128),
        hop_links.reshape(144 * ZL, 128),
        clover_inverse.reshape(144 * ZL, 128),
        momenta.T,
        mode_weights.reshape(1, NMODE),
        separations,
    )
    return odd_modes.reshape(even_modes.shape), correlator


def solution(mesh):
    in_specs = (
        P(None, None, None, None, "ta", "sa", None),
        P(None, None, None, None, None, "ta", "sa", None),
        P(None, None, None, None, "ta", "sa", None),
        P(),
        P(),
        P("ta", None),
    )
    out_specs = (P(None, None, None, None, "ta", "sa", None), P("ta", None))
    return jax.shard_map(
        functools.partial(body, mesh.shape["ta"], mesh.shape["sa"]),
        mesh=mesh,
        in_specs=in_specs,
        out_specs=out_specs,
        check_vma=False,
    )
```

time: 61.7 us -> 52 us (0.84)
  Pallas kernels: 57 us -> 48.8 us
  local copies, waits for them, and re-layouts: 3.84 us -> 2.39 us
    pallas_call x3 -> x1, Pallas kernels: 57 us -> 48.8 us  [body(): pl.pallas_call(functools.partial(kernel, nt, ns), out_shape=(shape((NMODE...]
    unnamed x14 -> x4, local copies, waits for them, and re-layouts: 3.84 us -> 2.39 us
where the time goes in v2:
time: 52 us; the launch traced here: 51.9 us
  Pallas kernels  48.8 us (94%)
  local copies, waits for them, and re-layouts  2.39 us (5%)
  between operations  0.65 us (1%)
    pallas_call x1, Pallas kernels, body(): pl.pallas_call(functools.partial(kernel, nt, ns), out_shape=(shape((NMODE...  48.8 us
    unnamed x4, local copies, waits for them, and re-layouts  2.39 us

profile of v2, /device:TPU:1, one launch (start us, length us, event | category | flops | bytes accessed | tf_op | source)
XLA Modules:
  0.0 51.9 jit_solution(13734278363378202347)
XLA Ops:
  0.6 48.8 %correlator.1 = (bf16[16,24,4,128]{3,2,1,0:T(4,128)(2,1)}, f32[1,16]{1,0:T(1,128)}) custom-call(bf16[1536,128]{1,0:T(8,128)(2,1)} %bitcast.8, bf16[576,128]{1,0:T(8,128)(2,1)} %bitcast.11, f32[576,128]{1,0:T(8,128)} %bitcast.10, s32[3,16]{1,0:T(4,128)} %bitcast.12, f32[1,16]{1,0:T(1,128)} %bitcast.13, s32[1,16]{1,0:T(1,128)} %sep_hbm.1), custom_call_target="tpu_custom_call" | custom-call | tf_op jit(solution)/shard_map/correlator/pallas_call | solution.py:499
  49.5 0.0 copy-start
  49.5 1.9 %copy.11 = bf16[16,2,4,3,1,4,128]{6,5,4,3,2,1,0:T(4,128)(2,1)} copy(bf16[16,2,4,3,1,4,128]{6,5,4,3,2,1,0:T(4,128)(2,1)} %bitcast.9) | data formatting | bytes 786432
  51.4 0.0 copy-done
  51.4 0.5 copy.12
Async XLA Ops:
  49.5 1.9 %copy-start = (f32[1,16]{1,0:T(1,128)S(1)}, f32[1,16]{1,0:T(1,128)}, u32[]{:S(2)}) copy-start(f32[1,16]{1,0:T(1,128)} %get-tuple-element.11) | copy-start | bytes 196

commit v3 on v2

--- a/solution.py
+++ b/solution.py
@@ -153,13 +153,32 @@
             )
 
 
+def plane_distance(step):
+    dy, dx, dn, dc = step
+    return -(min(dy, 4 - dy) + (2 * dx if not dn else 1)), -dc
+
+
+plane_steps = sorted(
+    [
+        (dy, dx, dn, dc)
+        for dy in range(4)
+        for dx in range(2)
+        for dn in range(2)
+        for dc in range(2)
+        if dy or dx or dn or dc
+    ],
+    key=plane_distance,
+)
+ring_steps = (4, 3, 5, 2, 6, 1, 7)
+
+
 def kernel(
     nt, ns,
     e_hbm, links_hbm, clover_hbm, momenta_hbm, weights_hbm, sep_hbm,
     odd_ref, out_ref,
     e_ref, links_ref, clover_ref, momenta_ref, weights_ref, sep_ref,
     ef, ewide, e2, st, sz, ht, hz, tf, zf, lf, of, ob, cos_ref, sin_ref,
-    total_ref, arr1, turn2, send2, arr2, gathered, send3, arr3, send4, arr4,
+    total_ref, arr1, turn2, send2, arr2, gathered, send3, arr3,
     in_sem, ts_sem, tr_sem, zs_sem, zr_sem, x_send, x_recv,
 ):
     t = lax.axis_index("ta")
@@ -168,16 +187,16 @@
     t_up, t_dn = lax.rem(t + 1, nt), lax.rem(t + nt - 1, nt)
     s_up, s_dn = lax.rem(s + 1, ns), lax.rem(s + ns - 1, ns)
     partners = ((t_dn, s), (t_up, s), (t, s_dn), (t, s_up))
-    mine_a = ty * 4 + s
-    mine_b = tz * 2 + tx
-
-    def member_a(index):
-        return tz * 8 + (index // 4) * 2 + tx, lax.rem(index, 4)
-
-    def member_b(index):
-        return (index // 2) * 8 + ty * 2 + lax.rem(index, 2), s
-
-    groups = ((mine_a, member_a), (mine_b, member_b))
+    place = lax.rem(t, 8) * 4 + s
+
+    def in_plane(step):
+        dy, dx, dn, dc = step
+        x_half, x_near, core = lax.rem(tx + dx, 2), lax.rem(s // 2 + dn, 2), lax.rem(s + dc, 2)
+        return tz * 8 + lax.rem(ty + dy, 4) * 2 + x_half, x_near * 2 + core
+
+    def along_planes(step):
+        return lax.rem(tz + step, 8) * 8 + lax.rem(t, 8), s
+
     loads = []
     for i, (source, target) in enumerate(
         (
@@ -191,14 +210,10 @@
     barrier = pltpu.get_barrier_semaphore()
     for partner in partners[:2]:
         pl.semaphore_signal(barrier, inc=1, device_id=partner, device_id_type=MESH)
-    for mine, member in groups:
-        def greet(d, carry, mine=mine, member=member):
-            pl.semaphore_signal(
-                barrier, inc=1, device_id=member(lax.rem(mine + d, 16)), device_id_type=MESH
-            )
-            return carry
-
-        lax.fori_loop(1, 16, greet, 0)
+    for step in plane_steps:
+        pl.semaphore_signal(barrier, inc=1, device_id=in_plane(step), device_id_type=MESH)
+    for step in ring_steps:
+        pl.semaphore_signal(barrier, inc=1, device_id=along_planes(step), device_id_type=MESH)
 
     loads[0].wait()
 
@@ -271,7 +286,7 @@
     for z in range(ZL):
         prepare(z)
         if z == 0:
-            pl.semaphore_wait(barrier, 32)
+            pl.semaphore_wait(barrier, 2 + 31 + 7)
             z_copy(0).start()
         for way in range(2):
             t_copy(way, z).start()
@@ -398,32 +413,27 @@
 
     lax.fori_loop(0, ZL, far_step, 0)
 
-    def send(stage, group, source, target):
-        mine, member = group
-
-        def one(d, carry):
-            other = lax.rem(mine + d, 16)
-            pltpu.make_async_remote_copy(
-                src_ref=source(other),
-                dst_ref=target.at[mine],
-                send_sem=x_send.at[stage],
-                recv_sem=x_recv.at[stage],
-                device_id=member(other),
-                device_id_type=MESH,
-            ).start()
-            return carry
-
-        lax.fori_loop(1, 16, one, 0)
-
-    def wait(stage, target, sems):
-        others = target.at[pl.ds(0, 15)]
+    def send(stage, source, target, slot, device):
+        pltpu.make_async_remote_copy(
+            src_ref=source,
+            dst_ref=target.at[slot],
+            send_sem=x_send.at[stage],
+            recv_sem=x_recv.at[stage],
+            device_id=device,
+            device_id_type=MESH,
+        ).start()
+
+    def wait(stage, target, count, sems):
+        others = target.at[pl.ds(0, count)]
         pltpu.make_async_copy(others, others, sems.at[stage]).wait()
 
-    def rows_a(index):
-        return pl.ds(pl.multiple_of(index * 16, 16), 16)
-
-    send(0, groups[0], lambda i: total_ref.at[rows_a(i)], arr1)
-    arr1[mine_a] = total_ref[rows_a(mine_a), :]
+    def rows_of(index):
+        return pl.ds(pl.multiple_of(index * 8, 8), 8)
+
+    for step in plane_steps:
+        device = in_plane(step)
+        send(0, total_ref.at[rows_of(lax.rem(device[0], 8) * 4 + device[1])], arr1, place, device)
+    arr1[place] = total_ref[rows_of(place), :]
 
     def turn(comp, carry):
         for z in range(ZL):
@@ -435,59 +445,71 @@
     lax.fori_loop(0, 24, turn, 0)
     loads[4].wait()
     loads[5].wait()
-    wait(0, arr1, x_recv)
-    for y in range(4):
-        field = arr1[4 * y] + arr1[4 * y + 1] + arr1[4 * y + 2] + arr1[4 * y + 3]
-        field = field.astype(BF16).astype(F32)
-        for g in range(2):
-            turn2[pl.ds(g * 32 + y, 8, stride=4), :] = field[g * 8 : g * 8 + 8]
-    for i in range(16):
-        send2[i] = turn2[pl.ds(i * 4, 4), :]
-    send(1, groups[1], lambda i: send2.at[i], arr2)
-    arr2[mine_b] = send2[mine_b]
     weights = weights_ref[...]
     lane16 = lax.broadcasted_iota(jnp.int32, (NMODE, 128), 1)
     spread = (lane16 % NMODE == lax.broadcasted_iota(jnp.int32, (NMODE, 128), 0)).astype(F32)
     weight_j = jnp.dot(weights, spread, precision=lax.Precision.HIGHEST, preferred_element_type=F32)
     mode = lax.broadcasted_iota(jnp.int32, (1, NMODE), 1)
-    weight_i = jnp.sum(jnp.where(mode == mine_b, weights, 0.0), axis=1, keepdims=True)
-    pair_weight = weight_i * weight_j
-    gathered[...] = jnp.zeros_like(gathered)
-    wait(1, arr2, x_recv)
-    for i in range(16):
-        gathered[pl.ds(i * 4, 4), :] = arr2[i]
-    everything = gathered[...]
+    pair_weights = [
+        jnp.sum(
+            jnp.where(mode == lax.rem(place, 2) * 8 + r, weights, 0.0), axis=1, keepdims=True
+        )
+        * weight_j
+        for r in range(8)
+    ]
+    across = lax.broadcasted_iota(jnp.int32, (16, 16), 1)
+    diagonal = across == lax.broadcasted_iota(jnp.int32, (16, 16), 0)
+    separation = jnp.sum(
+        jnp.where(diagonal, sep_ref[...].astype(F32), 0.0), axis=1, keepdims=True
+    ).astype(jnp.int32)
+    chosen = lax.broadcasted_iota(jnp.int32, (16, 128), 1) == lax.rem(t + separation, nt)
+    wait(0, arr1, 31, x_recv)
+    for j in range(8):
+        field = arr1[4 * j] + arr1[4 * j + 1] + arr1[4 * j + 2] + arr1[4 * j + 3]
+        turn2[pl.ds(j, 8, stride=8), :] = field
+    send2[...] = turn2[...].astype(BF16)
+    for step in ring_steps:
+        send(1, send2, arr2, tz, along_planes(step))
+    arr2[tz] = send2[...]
+    own = send2[...].astype(F32)
+    weighted = [own[8 * r : 8 * r + 8] * pair_weights[r] for r in range(8)]
+    high = [v.astype(BF16) for v in weighted]
+    low = [(v - h.astype(F32)).astype(BF16) for v, h in zip(weighted, high)]
+    sources = jnp.concatenate(
+        [jnp.concatenate(high, axis=1), jnp.concatenate(low, axis=1)], axis=0
+    )
+    wait(1, arr2, 7, x_recv)
+    planes = [arr2[i].astype(F32) for i in range(8)]
+    sinks = jnp.concatenate(
+        [
+            jnp.concatenate([planes[i][8 * r : 8 * r + 8] for i in range(8)], axis=0).astype(BF16)
+            for r in range(8)
+        ],
+        axis=1,
+    )
+    sinks = jnp.concatenate([sinks, sinks], axis=0)
     product = lax.dot_general(
-        everything[:64] * pair_weight,
-        everything,
-        (((1,), (1,)), ((), ())),
-        precision=lax.Precision.HIGHEST,
-        preferred_element_type=F32,
-    )
-    turn2[...] = product
-    for i in range(16):
-        send3[i] = turn2[pl.ds(i * 4, 4), :]
-    send(2, groups[1], lambda i: send3.at[i], arr3)
-    arr3[mine_b] = send3[mine_b]
-    wait(2, arr3, x_recv)
-    part = jnp.sum(arr3[...], axis=0)
-    for y in range(4):
-        send4[y] = part[y : y + 1]
-    send(3, groups[0], lambda i: send4.at[i // 4], arr4)
-    arr4[mine_a] = send4[ty]
-    sink = lax.rem(t + sep_ref[...], nt)
-    column = (sink // 8 * 2 + lax.rem(sink, 2)) * 4 + lax.rem(sink, 8) // 2
-    chosen = (lax.broadcasted_iota(jnp.int32, (128, 16), 0) == column).astype(F32)
-    wait(3, arr4, x_recv)
-    row = jnp.sum(arr4[...], axis=0)
-    picked = jnp.dot(row, chosen, precision=lax.Precision.HIGHEST, preferred_element_type=F32)
-    out_ref[...] = picked * (1.0 / (16.0 * NMODE * NMOM * LS**3))
+        sources, sinks, (((1,), (1,)), ((), ())), preferred_element_type=F32
+    )
+    gathered[...] = product[:8] + product[8:]
+    for j in range(8):
+        send3[j] = gathered[pl.ds(j, 1), :]
+    for step in plane_steps:
+        device = in_plane(step)
+        send(2, send3.at[lax.rem(device[0], 8)], arr3, place, device)
+    arr3[place] = send3[lax.rem(t, 8)]
+    wait(2, arr3, 31, x_recv)
+    row = jnp.sum(arr3[...], axis=0)
+    picked = jnp.sum(jnp.where(chosen, row, 0.0), axis=1, keepdims=True)
+    out_ref[...] = jnp.sum(jnp.where(diagonal, picked, 0.0), axis=0, keepdims=True) * (
+        1.0 / (16.0 * NMODE * NMOM * LS**3)
+    )
     for way in range(2):
         z_copy(way).wait_send()
         for z in range(ZL):
             t_copy(way, z).wait_send()
-    for stage, target in enumerate((arr1, arr2, arr3, arr4)):
-        wait(stage, target, x_send)
+    for stage, target, count in ((0, arr1, 31), (1, arr2, 7), (2, arr3, 31)):
+        wait(stage, target, count, x_send)
 
 
 def body(nt, ns, even_modes, hop_links, clover_inverse, momenta, mode_weights, separations):
@@ -523,16 +545,14 @@
             pltpu.VMEM((2, ZL, NMOM, 128), F32),
             pltpu.VMEM((2, ZL, NMOM, 128), F32),
             pltpu.VMEM((NMOM * NMODE, 128), F32),
-            pltpu.VMEM((16, 16, 128), F32),
+            pltpu.VMEM((32, 8, 128), F32),
             pltpu.VMEM((64, 128), F32),
-            pltpu.VMEM((16, 4, 128), F32),
-            pltpu.VMEM((16, 4, 128), F32),
-            pltpu.VMEM((128, 128), F32),
-            pltpu.VMEM((16, 4, 128), F32),
-            pltpu.VMEM((16, 4, 128), F32),
-            pltpu.VMEM((4, 1, 128), F32),
-            pltpu.VMEM((16, 1, 128), F32),
-            dma((6,)), dma((2, ZL)), dma((2, ZL)), dma((2,)), dma((2,)), dma((4,)), dma((4,)),
+            pltpu.VMEM((64, 128), BF16),
+            pltpu.VMEM((8, 64, 128), BF16),
+            pltpu.VMEM((8, 128), F32),
+            pltpu.VMEM((8, 1, 128), F32),
+            pltpu.VMEM((32, 1, 128), F32),
+            dma((6,)), dma((2, ZL)), dma((2, ZL)), dma((2,)), dma((2,)), dma((3,)), dma((3,)),
         ],
         compiler_params=pltpu.CompilerParams(
             collective_id=0, has_side_effects=True, vmem_limit_bytes=63 * 1024 * 1024

time: 52 us -> 46 us (0.88)
  Pallas kernels: 48.8 us -> 42.9 us
    pallas_call x1, Pallas kernels: 48.8 us -> 42.9 us  [body(): pl.pallas_call(functools.partial(kernel, nt, ns), out_shape=(shape((NMODE...]
where the time goes in v3:
time: 46 us; the launch traced here: 45.9 us
  Pallas kernels  42.9 us (93%)
  local copies, waits for them, and re-layouts  2.39 us (5%)
  between operations  0.65 us (1%)
    pallas_call x1, Pallas kernels, body(): pl.pallas_call(functools.partial(kernel, nt, ns), out_shape=(shape((NMODE...  42.9 us
    unnamed x4, local copies, waits for them, and re-layouts  2.39 us

profile of v3, /device:TPU:1, one launch (start us, length us, event | category | flops | bytes accessed | tf_op | source)
XLA Modules:
  0.0 45.9 jit_solution(11372563665284197004)
XLA Ops:
  0.6 42.9 %correlator.1 = (bf16[16,24,4,128]{3,2,1,0:T(4,128)(2,1)}, f32[1,16]{1,0:T(1,128)}) custom-call(bf16[1536,128]{1,0:T(8,128)(2,1)} %bitcast.8, bf16[576,128]{1,0:T(8,128)(2,1)} %bitcast.11, f32[576,128]{1,0:T(8,128)} %bitcast.10, s32[3,16]{1,0:T(4,128)} %bitcast.12, f32[1,16]{1,0:T(1,128)} %bitcast.13, s32[1,16]{1,0:T(1,128)} %sep_hbm.1), custom_call_target="tpu_custom_call" | custom-call | tf_op jit(solution)/shard_map/correlator/pallas_call | solution.py:521
  43.5 0.0 copy-start
  43.5 1.9 %copy.11 = bf16[16,2,4,3,1,4,128]{6,5,4,3,2,1,0:T(4,128)(2,1)} copy(bf16[16,2,4,3,1,4,128]{6,5,4,3,2,1,0:T(4,128)(2,1)} %bitcast.9) | data formatting | bytes 786432
  45.4 0.0 copy-done
  45.4 0.5 %copy.12 = f32[1,16]{1,0:T(1,128)} copy(f32[1,16]{1,0:T(1,128)S(1)} %copy-done) | data formatting | bytes 128
Async XLA Ops:
  43.5 1.9 %copy-start = (f32[1,16]{1,0:T(1,128)S(1)}, f32[1,16]{1,0:T(1,128)}, u32[]{:S(2)}) copy-start(f32[1,16]{1,0:T(1,128)} %get-tuple-element.11) | copy-start | bytes 196

commit v4 on v3

--- a/solution.py
+++ b/solution.py
@@ -283,14 +283,15 @@
                     ef[z, q * 12 + a * 3 + c] = both[a][c][q]
                     e2[z, q * 12 + a * 3 + c] = both[a][c][q].astype(BF16)
 
-    for z in range(ZL):
+    for z in (0, 3, 2, 1):
         prepare(z)
         if z == 0:
             pl.semaphore_wait(barrier, 2 + 31 + 7)
             z_copy(0).start()
+        if z == ZL - 1:
+            z_copy(1).start()
         for way in range(2):
             t_copy(way, z).start()
-    z_copy(1).start()
 
     loads[1].wait()
     phase_tables(t, s, momenta_ref[...], cos_ref, sin_ref)
@@ -375,7 +376,8 @@
     lax.fori_loop(0, 2 * ZL, near_step, 0)
     loads[3].wait()
 
-    def far_step(z, carry):
+    def far_step(i, carry):
+        z = lax.rem(3 * i, ZL)
         for way in range(2):
             t_copy(way, z).wait_recv()
             tf[way] = ht[way, z].astype(F32)
@@ -520,7 +522,7 @@
     sites = (ZL, 24, NMODE, 128)
     odd_modes, correlator = pl.pallas_call(
         functools.partial(kernel, nt, ns),
-        out_shape=(shape((NMODE, 24, ZL, 128), BF16), shape((1, 16), F32)),
+        out_shape=(pltpu.VMEM((NMODE, 24, ZL, 128), BF16), pltpu.VMEM((1, 16), F32)),
         in_specs=[hbm] * 6,
         out_specs=(vmem, vmem),
         scratch_shapes=[

time: 46 us -> 41.1 us (0.89)
  Pallas kernels: 42.9 us -> 39.1 us
  local copies, waits for them, and re-layouts: 2.39 us -> 1.26 us
    pallas_call x1, Pallas kernels: 42.9 us -> 39.1 us  [body(): pl.pallas_call(functools.partial(kernel, nt, ns), out_shape=(pltpu.VMEM((...]
    unnamed x4 -> x2, local copies, waits for them, and re-layouts: 2.39 us -> 1.26 us
where the time goes in v4:
time: 41.1 us; the launch traced here: 41 us
  Pallas kernels  39.1 us (95%)
  local copies, waits for them, and re-layouts  1.26 us (3%)
  between operations  0.64 us (2%)
    pallas_call x1, Pallas kernels, body(): pl.pallas_call(functools.partial(kernel, nt, ns), out_shape=(pltpu.VMEM((...  39.1 us
    unnamed x2, local copies, waits for them, and re-layouts  1.26 us

profile of v4, /device:TPU:1, one launch (start us, length us, event | category | flops | bytes accessed | tf_op | source)
XLA Modules:
  0.0 41.0 jit_solution(18536116905852165)
XLA Ops:
  0.6 39.1 %correlator.1 = (bf16[16,24,4,128]{3,2,1,0:T(4,128)(2,1)S(1)}, f32[1,16]{1,0:T(1,128)S(1)}) custom-call(bf16[1536,128]{1,0:T(8,128)(2,1)} %bitcast.9, bf16[576,128]{1,0:T(8,128)(2,1)} %bitcast.11, f32[576,128]{1,0:T(8,128)} %bitcast.10, s32[3,16]{1,0:T(4,128)} %bitcast.12, f32[1,16]{1,0:T(1,128)} %bitcast.13, s32[1,16]{1,0:T(1,128)} %sep_hbm.1), custom_call_target="tpu_custom_call" | custom-call | tf_op jit(solution)/shard_map/correlator/pallas_call | solution.py:523
  39.8 0.7 %copy.11 = bf16[16,2,4,3,1,4,128]{6,5,4,3,2,1,0:T(4,128)(2,1)} copy(bf16[16,2,4,3,1,4,128]{6,5,4,3,2,1,0:T(4,128)(2,1)S(1)} %bitcast.8) | data formatting | bytes 786432
  40.5 0.5 %copy.12 = f32[1,16]{1,0:T(1,128)} copy(f32[1,16]{1,0:T(1,128)S(1)} %get-tuple-element.9) | data formatting | bytes 128

commit v5 on v4

--- a/solution.py
+++ b/solution.py
@@ -179,7 +179,7 @@
     e_ref, links_ref, clover_ref, momenta_ref, weights_ref, sep_ref,
     ef, ewide, e2, st, sz, ht, hz, tf, zf, lf, of, ob, cos_ref, sin_ref,
     total_ref, arr1, turn2, send2, arr2, gathered, send3, arr3,
-    in_sem, ts_sem, tr_sem, zs_sem, zr_sem, x_send, x_recv,
+    e_sem, in_sem, ts_sem, tr_sem, zs_sem, zr_sem, x_send, x_recv,
 ):
     t = lax.axis_index("ta")
     s = lax.axis_index("sa")
@@ -198,10 +198,16 @@
         return lax.rem(tz + step, 8) * 8 + lax.rem(t, 8), s
 
     loads = []
+    e_loads = []
+    for i in range(4):
+        part = pl.ds(i * 384, 384)
+        load = pltpu.make_async_copy(e_hbm.at[part], e_ref.at[part], e_sem.at[i])
+        load.start()
+        e_loads.append(load)
     for i, (source, target) in enumerate(
         (
-            (e_hbm, e_ref), (momenta_hbm, momenta_ref), (links_hbm, links_ref),
-            (clover_hbm, clover_ref), (weights_hbm, weights_ref), (sep_hbm, sep_ref),
+            (momenta_hbm, momenta_ref), (links_hbm, links_ref), (clover_hbm, clover_ref),
+            (weights_hbm, weights_ref), (sep_hbm, sep_ref),
         )
     ):
         load = pltpu.make_async_copy(source, target, in_sem.at[i])
@@ -210,19 +216,16 @@
     barrier = pltpu.get_barrier_semaphore()
     for partner in partners[:2]:
         pl.semaphore_signal(barrier, inc=1, device_id=partner, device_id_type=MESH)
-    for step in plane_steps:
-        pl.semaphore_signal(barrier, inc=1, device_id=in_plane(step), device_id_type=MESH)
+    plane_devices = [in_plane(step) for step in plane_steps]
+    for device in plane_devices:
+        pl.semaphore_signal(barrier, inc=1, device_id=device, device_id_type=MESH)
     for step in ring_steps:
         pl.semaphore_signal(barrier, inc=1, device_id=along_planes(step), device_id_type=MESH)
 
-    loads[0].wait()
-
-    def widen(m, carry):
-        rows = pl.ds(pl.multiple_of(m * 96, 96), 96)
-        ewide[rows, :] = e_ref[rows, :].astype(F32)
-        return carry
-
-    lax.fori_loop(0, NMODE, widen, 0)
+    for i, load in enumerate(e_loads):
+        load.wait()
+        part = pl.ds(i * 384, 384)
+        ewide[part, :] = e_ref[part, :].astype(F32)
     sign_dn = jnp.where(t == 0, -1.0, 1.0).astype(F32)
     sign_up = jnp.where(t == nt - 1, -1.0, 1.0).astype(F32)
 
@@ -293,7 +296,7 @@
         for way in range(2):
             t_copy(way, z).start()
 
-    loads[1].wait()
+    loads[0].wait()
     phase_tables(t, s, momenta_ref[...], cos_ref, sin_ref)
     total_ref[...] = jnp.zeros_like(total_ref)
 
@@ -302,7 +305,7 @@
         return carry
 
     lax.fori_loop(0, ZL, even_step, 0)
-    loads[2].wait()
+    loads[1].wait()
 
     def widen_links(i, carry):
         rows = pl.ds(pl.multiple_of(i * 96, 96), 96)
@@ -374,7 +377,7 @@
         return carry
 
     lax.fori_loop(0, 2 * ZL, near_step, 0)
-    loads[3].wait()
+    loads[2].wait()
 
     def far_step(i, carry):
         z = lax.rem(3 * i, ZL)
@@ -432,8 +435,7 @@
     def rows_of(index):
         return pl.ds(pl.multiple_of(index * 8, 8), 8)
 
-    for step in plane_steps:
-        device = in_plane(step)
+    for device in plane_devices:
         send(0, total_ref.at[rows_of(lax.rem(device[0], 8) * 4 + device[1])], arr1, place, device)
     arr1[place] = total_ref[rows_of(place), :]
 
@@ -445,8 +447,8 @@
         return carry
 
     lax.fori_loop(0, 24, turn, 0)
+    loads[3].wait()
     loads[4].wait()
-    loads[5].wait()
     weights = weights_ref[...]
     lane16 = lax.broadcasted_iota(jnp.int32, (NMODE, 128), 1)
     spread = (lane16 % NMODE == lax.broadcasted_iota(jnp.int32, (NMODE, 128), 0)).astype(F32)
@@ -465,6 +467,10 @@
         jnp.where(diagonal, sep_ref[...].astype(F32), 0.0), axis=1, keepdims=True
     ).astype(jnp.int32)
     chosen = lax.broadcasted_iota(jnp.int32, (16, 128), 1) == lax.rem(t + separation, nt)
+    for way in range(2):
+        z_copy(way).wait_send()
+        for z in range(ZL):
+            t_copy(way, z).wait_send()
     wait(0, arr1, 31, x_recv)
     for j in range(8):
         field = arr1[4 * j] + arr1[4 * j + 1] + arr1[4 * j + 2] + arr1[4 * j + 3]
@@ -480,6 +486,8 @@
     sources = jnp.concatenate(
         [jnp.concatenate(high, axis=1), jnp.concatenate(low, axis=1)], axis=0
     )
+    gathered[...] = jnp.zeros_like(gathered)
+    wait(0, arr1, 31, x_send)
     wait(1, arr2, 7, x_recv)
     planes = [arr2[i].astype(F32) for i in range(8)]
     sinks = jnp.concatenate(
@@ -489,29 +497,34 @@
         ],
         axis=1,
     )
-    sinks = jnp.concatenate([sinks, sinks], axis=0)
     product = lax.dot_general(
         sources, sinks, (((1,), (1,)), ((), ())), preferred_element_type=F32
     )
-    gathered[...] = product[:8] + product[8:]
+    gathered[:, :64] = product[:8] + product[8:]
     for j in range(8):
         send3[j] = gathered[pl.ds(j, 1), :]
-    for step in plane_steps:
-        device = in_plane(step)
+    for device in plane_devices:
         send(2, send3.at[lax.rem(device[0], 8)], arr3, place, device)
     arr3[place] = send3[lax.rem(t, 8)]
+    wait(1, arr2, 7, x_send)
     wait(2, arr3, 31, x_recv)
     row = jnp.sum(arr3[...], axis=0)
     picked = jnp.sum(jnp.where(chosen, row, 0.0), axis=1, keepdims=True)
     out_ref[...] = jnp.sum(jnp.where(diagonal, picked, 0.0), axis=0, keepdims=True) * (
         1.0 / (16.0 * NMODE * NMOM * LS**3)
     )
-    for way in range(2):
-        z_copy(way).wait_send()
-        for z in range(ZL):
-            t_copy(way, z).wait_send()
-    for stage, target, count in ((0, arr1, 31), (1, arr2, 7), (2, arr3, 31)):
-        wait(stage, target, count, x_send)
+    wait(2, arr3, 31, x_send)
+
+
+def finish_kernel(odd_ref, row_ref, odd_out, row_out, sems):
+    copies = [
+        pltpu.make_async_copy(odd_ref, odd_out, sems.at[0]),
+        pltpu.make_async_copy(row_ref, row_out, sems.at[1]),
+    ]
+    for copy in copies:
+        copy.start()
+    for copy in copies:
+        copy.wait()
 
 
 def body(nt, ns, even_modes, hop_links, clover_inverse, momenta, mode_weights, separations):
@@ -554,7 +567,7 @@
             pltpu.VMEM((8, 128), F32),
             pltpu.VMEM((8, 1, 128), F32),
             pltpu.VMEM((32, 1, 128), F32),
-            dma((6,)), dma((2, ZL)), dma((2, ZL)), dma((2,)), dma((2,)), dma((3,)), dma((3,)),
+            dma((4,)), dma((5,)), dma((2, ZL)), dma((2, ZL)), dma((2,)), dma((2,)), dma((3,)), dma((3,)),
         ],
         compiler_params=pltpu.CompilerParams(
             collective_id=0, has_side_effects=True, vmem_limit_bytes=63 * 1024 * 1024
@@ -568,6 +581,15 @@
         mode_weights.reshape(1, NMODE),
         separations,
     )
+    odd_modes, correlator = pl.pallas_call(
+        finish_kernel,
+        out_shape=(shape(odd_modes.shape, BF16), shape((1, 16), F32)),
+        in_specs=[vmem, vmem],
+        out_specs=(hbm, hbm),
+        scratch_shapes=[dma((2,))],
+        compiler_params=pltpu.CompilerParams(vmem_limit_bytes=1024 * 1024),
+        name="finish",
+    )(odd_modes, correlator)
     return odd_modes.reshape(even_modes.shape), correlator
 
 

time: 41.1 us -> 40.6 us (0.988)
  local copies, waits for them, and re-layouts: 1.26 us -> 0 us
  Pallas kernels: 39.1 us -> 39.8 us
    unnamed x2 -> x0, local copies, waits for them, and re-layouts: 1.26 us -> none
    pallas_call x0 -> x1, Pallas kernels: none -> 0.77 us  [body(): pl.pallas_call(finish_kernel, out_shape=(shape(odd_modes.shape, BF16), sh...]
where the time goes in v5:
time: 40.6 us; the launch traced here: 40.5 us
  Pallas kernels  39.8 us (98%)
  between operations  0.64 us (2%)
    pallas_call x1, Pallas kernels, body(): pl.pallas_call(functools.partial(kernel, nt, ns), out_shape=(pltpu.VMEM((...  39.1 us

profile of v5, /device:TPU:1, one launch (start us, length us, event | category | flops | bytes accessed | tf_op | source)
XLA Modules:
  0.0 40.5 jit_solution(579814656812934405)
XLA Ops:
  0.6 39.1 %correlator.1 = (bf16[16,24,4,128]{3,2,1,0:T(4,128)(2,1)S(1)}, f32[1,16]{1,0:T(1,128)S(1)}) custom-call(bf16[1536,128]{1,0:T(8,128)(2,1)} %bitcast.8, bf16[576,128]{1,0:T(8,128)(2,1)} %bitcast.10, f32[576,128]{1,0:T(8,128)} %bitcast.9, s32[3,16]{1,0:T(4,128)} %bitcast.11, f32[1,16]{1,0:T(1,128)} %bitcast.12, s32[1,16]{1,0:T(1,128)} %sep_hbm.1), custom_call_target="tpu_custom_call" | custom-call | tf_op jit(solution)/shard_map/correlator/pallas_call | solution.py:536
  39.7 0.8 %finish.1 = (bf16[16,24,4,128]{3,2,1,0:T(4,128)(2,1)}, f32[1,16]{1,0:T(1,128)}) custom-call(bf16[16,24,4,128]{3,2,1,0:T(4,128)(2,1)S(1)} %get-tuple-element.6.odd_ref, f32[1,16]{1,0:T(1,128)S(1)} %get-tuple-element.7.row_ref), custom_call_target="tpu_custom_call" | custom-call | tf_op jit(solution)/shard_map/finish/pallas_call | solution.py:584

commit v6 on v5

--- a/solution.py
+++ b/solution.py
@@ -475,7 +475,7 @@
     for j in range(8):
         field = arr1[4 * j] + arr1[4 * j + 1] + arr1[4 * j + 2] + arr1[4 * j + 3]
         turn2[pl.ds(j, 8, stride=8), :] = field
-    send2[...] = turn2[...].astype(BF16)
+    send2[...] = turn2[pl.ds(0, 64), :].astype(BF16)
     for step in ring_steps:
         send(1, send2, arr2, tz, along_planes(step))
     arr2[tz] = send2[...]
@@ -546,7 +546,7 @@
             pltpu.VMEM((1, NMODE), F32),
             pltpu.VMEM((1, 16), jnp.int32),
             pltpu.VMEM(sites, F32),
-            pltpu.VMEM((NMODE * 24 * ZL, 128), F32),
+            pltpu.VMEM(((NMODE + 1) * 24 * ZL, 128), F32),
             pltpu.VMEM(sites, BF16),
             pltpu.VMEM((2, ZL, 12, NMODE, 128), BF16),
             pltpu.VMEM((2, 12, NMODE, 128), BF16),
@@ -561,7 +561,7 @@
             pltpu.VMEM((2, ZL, NMOM, 128), F32),
             pltpu.VMEM((NMOM * NMODE, 128), F32),
             pltpu.VMEM((32, 8, 128), F32),
-            pltpu.VMEM((64, 128), F32),
+            pltpu.VMEM((72, 128), F32),
             pltpu.VMEM((64, 128), BF16),
             pltpu.VMEM((8, 64, 128), BF16),
             pltpu.VMEM((8, 128), F32),

time: 40.6 us -> 40.6 us (level)
  no operation moved by 1% of the time
where the time goes in v6:
time: 40.6 us; the launch traced here: 40.5 us
  Pallas kernels  39.8 us (98%)
  between operations  0.64 us (2%)
    pallas_call x1, Pallas kernels, body(): pl.pallas_call(functools.partial(kernel, nt, ns), out_shape=(pltpu.VMEM((...  39.1 us

profile of v6, /device:TPU:1, one launch (start us, length us, event | category | flops | bytes accessed | tf_op | source)
XLA Modules:
  0.0 40.5 jit_solution(4082947086796833333)
XLA Ops:
  0.6 39.1 %correlator.1 = (bf16[16,24,4,128]{3,2,1,0:T(4,128)(2,1)S(1)}, f32[1,16]{1,0:T(1,128)S(1)}) custom-call(bf16[1536,128]{1,0:T(8,128)(2,1)} %bitcast.8, bf16[576,128]{1,0:T(8,128)(2,1)} %bitcast.10, f32[576,128]{1,0:T(8,128)} %bitcast.9, s32[3,16]{1,0:T(4,128)} %bitcast.11, f32[1,16]{1,0:T(1,128)} %bitcast.12, s32[1,16]{1,0:T(1,128)} %sep_hbm.1), custom_call_target="tpu_custom_call" | custom-call | tf_op jit(solution)/shard_map/correlator/pallas_call | solution.py:536
  39.7 0.8 %finish.1 = (bf16[16,24,4,128]{3,2,1,0:T(4,128)(2,1)}, f32[1,16]{1,0:T(1,128)}) custom-call(bf16[16,24,4,128]{3,2,1,0:T(4,128)(2,1)S(1)} %get-tuple-element.6.odd_ref, f32[1,16]{1,0:T(1,128)S(1)} %get-tuple-element.7.row_ref), custom_call_target="tpu_custom_call" | custom-call | tf_op jit(solution)/shard_map/finish/pallas_call | solution.py:584

commit v7 on v6

--- a/solution.py
+++ b/solution.py
@@ -111,16 +111,17 @@
             sin_ref[parity, zl] = circle((step + 12) & 15)
 
 
-def meson_part(modes_ref, parity, z, cos_ref, sin_ref, total_ref):
+def meson_part(modes_ref, parity, z, cos_ref, sin_ref, total_ref, p0=0, count=NMOM):
+    first = p0 * NMODE if isinstance(p0, int) else pl.multiple_of(p0 * NMODE, 128)
     for a in range(4):
         for c in range(3):
             comp = a * 3 + c
             vr = modes_ref[z, comp].astype(F32)
             vi = modes_ref[z, 12 + comp].astype(F32)
             rows = []
-            for p in range(NMOM):
-                cs = cos_ref[parity, z, pl.ds(p, 1), :]
-                sn = sin_ref[parity, z, pl.ds(p, 1), :]
+            for p in range(count):
+                cs = cos_ref[parity, z, pl.ds(p0 + p, 1), :]
+                sn = sin_ref[parity, z, pl.ds(p0 + p, 1), :]
                 rows.append(
                     jnp.concatenate(
                         [
@@ -148,7 +149,7 @@
                 real_rows.append(jnp.concatenate([gr, -gi], axis=1))
                 imag_rows.append(jnp.concatenate([gi, gr], axis=1))
             right = jnp.concatenate(real_rows + imag_rows, axis=0)
-            total_ref[...] += lax.dot_general(
+            total_ref[pl.ds(first, count * NMODE), :] += lax.dot_general(
                 left, right, (((1,), (1,)), ((), ())), preferred_element_type=F32
             )
 
@@ -379,8 +380,7 @@
     lax.fori_loop(0, 2 * ZL, near_step, 0)
     loads[2].wait()
 
-    def far_step(i, carry):
-        z = lax.rem(3 * i, ZL)
+    def far_hops(z):
         for way in range(2):
             t_copy(way, z).wait_recv()
             tf[way] = ht[way, z].astype(F32)
@@ -413,10 +413,15 @@
 
         lax.fori_loop(0, 2, group_step, 0)
         ob[z] = of[z].astype(BF16)
+
+    def far_step(i, carry):
+        z = lax.rem(3 * i, ZL)
+        far_hops(z)
         meson_part(ob, 1, z, cos_ref, sin_ref, total_ref)
         return carry
 
-    lax.fori_loop(0, ZL, far_step, 0)
+    lax.fori_loop(0, ZL - 1, far_step, 0)
+    far_hops(1)
 
     def send(stage, source, target, slot, device):
         pltpu.make_async_remote_copy(
@@ -435,8 +440,19 @@
     def rows_of(index):
         return pl.ds(pl.multiple_of(index * 8, 8), 8)
 
-    for device in plane_devices:
-        send(0, total_ref.at[rows_of(lax.rem(device[0], 8) * 4 + device[1])], arr1, place, device)
+    pair = ty - 2 * (ty // 2)
+    for half, rows in (
+        (1 - ty // 2, (lax.rem(ty + 2, 4), lax.rem(ty + 2, 4) + 1 - 2 * pair)),
+        (ty // 2, (ty + 1 - 2 * pair, ty)),
+    ):
+        meson_part(ob, 1, 1, cos_ref, sin_ref, total_ref, half * 8, 8)
+        for y in rows:
+            for dx, dn, dc in ((1, 0, 1), (1, 0, 0), (0, 1, 1), (0, 1, 0), (1, 1, 1), (1, 1, 0), (0, 0, 1), (0, 0, 0)):
+                if y is ty and not (dx or dn or dc):
+                    continue
+                x_half, x_near, core = lax.rem(tx + dx, 2), lax.rem(s // 2 + dn, 2), lax.rem(s + dc, 2)
+                device = (tz * 8 + y * 2 + x_half, x_near * 2 + core)
+                send(0, total_ref.at[rows_of((y * 2 + x_half) * 4 + device[1])], arr1, place, device)
     arr1[place] = total_ref[rows_of(place), :]
 
     def turn(comp, carry):

time: 40.6 us -> 40.5 us (level)
  no operation moved by 1% of the time
where the time goes in v7:
time: 40.5 us; the launch traced here: 40.4 us
  Pallas kernels  39.8 us (98%)
  between operations  0.64 us (2%)
    pallas_call x1, Pallas kernels, body(): pl.pallas_call(functools.partial(kernel, nt, ns), out_shape=(pltpu.VMEM((...  39 us

profile of v7, /device:TPU:1, one launch (start us, length us, event | category | flops | bytes accessed | tf_op | source)
XLA Modules:
  0.0 40.4 jit_solution(6162845805528355962)
XLA Ops:
  0.6 39.0 %correlator.1 = (bf16[16,24,4,128]{3,2,1,0:T(4,128)(2,1)S(1)}, f32[1,16]{1,0:T(1,128)S(1)}) custom-call(bf16[1536,128]{1,0:T(8,128)(2,1)} %bitcast.8, bf16[576,128]{1,0:T(8,128)(2,1)} %bitcast.10, f32[576,128]{1,0:T(8,128)} %bitcast.9, s32[3,16]{1,0:T(4,128)} %bitcast.11, f32[1,16]{1,0:T(1,128)} %bitcast.12, s32[1,16]{1,0:T(1,128)} %sep_hbm.1), custom_call_target="tpu_custom_call" | custom-call | tf_op jit(solution)/shard_map/correlator/pallas_call | solution.py:552
  39.6 0.8 %finish.1 = (bf16[16,24,4,128]{3,2,1,0:T(4,128)(2,1)}, f32[1,16]{1,0:T(1,128)}) custom-call(bf16[16,24,4,128]{3,2,1,0:T(4,128)(2,1)S(1)} %get-tuple-element.6.odd_ref, f32[1,16]{1,0:T(1,128)S(1)} %get-tuple-element.7.row_ref), custom_call_target="tpu_custom_call" | custom-call | tf_op jit(solution)/shard_map/finish/pallas_call | solution.py:600
